TPU v7x, 32 devices: a whole 2x2x4 slice. The times are simulated.
32 devices in a mesh: expert: 8 (over z, y), shard: 4 (over x, core).
Axes of the slice: x: 2, y: 2, z: 4, core: 2. Of those that a mesh axis runs over, the one named last changes fastest.
Arguments:
- residual_in: float32 [32768, 768], P(('expert', 'shard')), may hold values from -6 to 6
- norm1_gain: float32 [768], replicated, may hold values from 0.1 to 1.9
- w_projection: bfloat16 [768, 2304], P('shard'), may hold values from -0.21875 to 0.21875
- rel_bias: float32 [12, 32], replicated, may hold values from -3 to 3
- w_attn_out: bfloat16 [768, 768], P('shard'), may hold values from -0.625 to 0.625
- norm2_gain: float32 [768], replicated, may hold values from 0.1 to 1.9
- w_router: bfloat16 [768, 8], replicated, may hold values from -0.109375 to 0.109375
- expert_in: bfloat16 [8, 768, 3072], P('expert', None, 'shard'), may hold values from -0.21875 to 0.21875
- expert_out: bfloat16 [8, 3072, 768], P('expert', 'shard'), may hold values from -0.15625 to 0.15625
- segments: int32 [32, 1024], P(('expert', 'shard')), may hold values from 0 to 63, never falling along the last dimension, each value on 1 to 512 neighbouring positions
- routes: int32 [32768, 2], P(('expert', 'shard')), may hold values from 0 to 7, all different within a row; in each aligned block of 1024 rows (0 to 1023, 1024 to 2047, ...) at most 320 rows name the same one
- out_grad: float32 [32768, 768], P(('expert', 'shard')), may hold values from -6 to 6
Outputs:
- block_out: float32 [32768, 768], P(('expert', 'shard'))
- residual_grad: float32 [32768, 768], P(('expert', 'shard'))
- norm1_gain_grad: float32 [768], replicated
- projection_grad: float32 [768, 2304], P('shard')
- rel_bias_grad: float32 [12, 32], replicated
- attn_out_grad: float32 [768, 768], P('shard')
- norm2_gain_grad: float32 [768], replicated
- router_grad: float32 [768, 8], replicated
- expert_in_grad: float32 [8, 768, 3072], P('expert', None, 'shard')
- expert_out_grad: float32 [8, 3072, 768], P('expert', 'shard')
Inputs may be any that keep to these rules, and one draw needn't show every extreme that they name: `segments`: along each sequence the numbers never fall; each document spans 1 to 512 positions, and one spans exactly that many. `routes`: each token names two different experts. Among the rows of one device no expert is named more than 320 times, and in every draw some expert is named exactly 320 times by the rows of some device.
All inputs are finite; a program needn't handle non-finite values.
Results may differ from a plain program's by a relative error of at most 0.017.
Values may be sent and summed in bfloat16 or wider, within the bound.
A program may use at most 448 MiB of HBM per device.

v0:
```python
import jax
import jax.numpy as jnp
from jax import lax
from jax.sharding import PartitionSpec as P

epsilon = 1e-06
bucket_borders = (19, 21, 24, 27, 31, 35, 40, 46, 52, 59, 67, 77, 87, 99, 113)


def bucket_of(distance):
    beyond = jnp.zeros_like(distance)
    for border in bucket_borders:
        beyond = beyond + (distance >= border).astype(jnp.int32)
    return jnp.where(distance < 16, distance, 16 + beyond)


def rms_scale(values):
    return lax.rsqrt(jnp.mean(values * values, axis=-1, keepdims=True) + epsilon)


def norm_back(values, scale, gain, gradient):
    weighted = gradient * gain
    gain_grad = jnp.sum(gradient * values * scale, axis=0)
    inner = jnp.mean(weighted * values, axis=-1, keepdims=True)
    return (scale * weighted - values * scale * scale * scale * inner, gain_grad)


def add_rows(total, part):
    return total + part


def block_geometry(index, block_rows, seq_len, marks):
    start = index * block_rows
    sequence_start = start // seq_len * seq_len
    offset = start - sequence_start
    distance = (
        offset
        + jnp.arange(block_rows, dtype=jnp.int32)[:, None]
        - jnp.arange(seq_len, dtype=jnp.int32)[None, :]
    )
    mark_query = lax.dynamic_slice_in_dim(marks, start, block_rows, 0)
    allowed = (distance >= 0) & (mark_query[:, None] == marks[None, :])
    return (start, sequence_start, offset, allowed)


def skewed_bias(diagonal_bias, offset, block_rows, seq_len):
    heads = diagonal_bias.shape[0]
    wide = 2 * seq_len
    tiled = jnp.tile(diagonal_bias, (1, block_rows))[:, : block_rows * (wide - 1)]
    sheared = tiled.reshape(heads, block_rows, wide - 1)
    return lax.dynamic_slice_in_dim(sheared, seq_len - 1 - offset, seq_len, 2)


def diagonal_sums(score_grad, offset, seq_len):
    heads, block_rows, _ = score_grad.shape
    wide = 2 * seq_len
    placed = jnp.zeros((heads, block_rows, wide - 1), score_grad.dtype)
    placed = lax.dynamic_update_slice_in_dim(placed, score_grad, seq_len - 1 - offset, 2)
    flat = placed.reshape(heads, block_rows * (wide - 1))
    flat = jnp.concatenate([flat, jnp.zeros((heads, block_rows), score_grad.dtype)], axis=1)
    return jnp.sum(flat.reshape(heads, block_rows, wide), axis=1, dtype=jnp.float32)


def block_scores(query, keys_seq, bias_block, allowed, scale):
    raw = jnp.einsum("qhd,khd->hqk", query, keys_seq, preferred_element_type=jnp.float32)
    return jnp.where(allowed[None], raw * scale + bias_block, -1e30)


def slot_positions(flat_routes, experts_all):
    count = flat_routes.shape[0]
    width_blk = min(256, count)
    groups = count // width_blk
    member = flat_routes[:, None] == jnp.arange(experts_all, dtype=jnp.int32)[None, :]
    member_low = member.astype(jnp.bfloat16).reshape(groups, width_blk, experts_all)
    lower = (
        jnp.arange(width_blk, dtype=jnp.int32)[:, None]
        > jnp.arange(width_blk, dtype=jnp.int32)[None, :]
    ).astype(jnp.bfloat16)
    inside = jnp.einsum("rs,gse->gre", lower, member_low, preferred_element_type=jnp.float32)
    totals = jnp.sum(member_low.astype(jnp.float32), axis=1)
    before = jnp.cumsum(totals, axis=0) - totals
    earlier = (inside + before[:, None, :]).reshape(count, experts_all)
    position = jnp.sum(earlier * member.astype(jnp.float32), axis=1)
    return position.astype(jnp.int32)


def per_device(
    residual_in,
    norm1_gain,
    w_projection,
    rel_bias,
    w_attn_out,
    norm2_gain,
    w_router,
    expert_in,
    expert_out,
    segments,
    routes,
    out_grad,
):
    highest = lax.Precision.HIGHEST
    tokens_here, width = residual_in.shape
    heads, buckets = rel_bias.shape
    head_dim = width // heads
    seq_len = segments.shape[1]
    block_rows = min(512, seq_len)
    blocks = tokens_here // block_rows
    scale = head_dim ** (-0.5)
    experts_all = w_router.shape[1]
    capacity = max(2, 5 * tokens_here // (2 * experts_all))
    marks = segments.reshape(-1)
    full_projection, full_attn_out = (
        lax.all_gather(w_projection, "shard", axis=0, tiled=True),
        lax.all_gather(w_attn_out, "shard", axis=0, tiled=True),
    )
    scale1 = rms_scale(residual_in)
    normed = (residual_in * scale1 * norm1_gain).astype(jnp.bfloat16)
    projected = jnp.dot(normed, full_projection, preferred_element_type=jnp.float32).astype(
        jnp.bfloat16
    )
    queries = projected[:, :width].reshape(tokens_here, heads, head_dim)
    keys = projected[:, width : 2 * width].reshape(tokens_here, heads, head_dim)
    values = projected[:, 2 * width :].reshape(tokens_here, heads, head_dim)
    diag_distance = jnp.clip(seq_len - 1 - jnp.arange(2 * seq_len, dtype=jnp.int32), 0, seq_len - 1)
    bucket_table = (
        bucket_of(diag_distance)[:, None] == jnp.arange(buckets, dtype=jnp.int32)[None, :]
    ).astype(jnp.float32)
    diagonal_bias = jnp.dot(rel_bias, bucket_table.T, precision=highest)

    def forward_block(index):
        start, sequence_start, offset, allowed = block_geometry(index, block_rows, seq_len, marks)
        query = lax.dynamic_slice_in_dim(queries, start, block_rows, 0)
        bias_block = skewed_bias(diagonal_bias, offset, block_rows, seq_len)
        scores = block_scores(query, keys, bias_block, allowed, scale)
        peak = jnp.max(scores, axis=2, keepdims=True)
        weights = jnp.exp(scores - peak)
        totals = jnp.sum(weights, axis=2, keepdims=True)
        shares = (weights / totals).astype(jnp.bfloat16)
        mixed = jnp.einsum("hqk,khd->qhd", shares, values, preferred_element_type=jnp.float32)
        return (mixed, (peak + jnp.log(totals))[:, :, 0])

    mixed, log_totals = lax.map(forward_block, jnp.arange(blocks))
    merged = mixed.reshape(tokens_here, width).astype(jnp.bfloat16)
    attended = jnp.dot(merged, full_attn_out, preferred_element_type=jnp.float32)
    hidden = residual_in + attended
    scale2 = rms_scale(hidden)
    normed2 = (hidden * scale2 * norm2_gain).astype(jnp.bfloat16)
    logits = jnp.dot(normed2, w_router, preferred_element_type=jnp.float32)
    chosen = (routes[:, :, None] == jnp.arange(experts_all, dtype=jnp.int32)[None, None, :]).astype(
        jnp.float32
    )
    picked = jnp.sum(chosen * logits[:, None, :], axis=2)
    gates = jax.nn.softmax(picked, axis=-1)
    flat_routes = routes.reshape(-1)
    slot = flat_routes * capacity + slot_positions(flat_routes, experts_all)
    owner = jnp.full((experts_all * capacity,), 2 * tokens_here, jnp.int32)
    owner = owner.at[slot].set(jnp.arange(2 * tokens_here, dtype=jnp.int32))
    padded_rows = jnp.concatenate([normed2, jnp.zeros((1, width), jnp.bfloat16)], axis=0)
    outgoing = padded_rows[owner // 2].reshape(experts_all, capacity, width)
    arrived = lax.all_to_all(outgoing, "expert", split_axis=0, concat_axis=0, tiled=True)
    inner = expert_in[0]
    outer = expert_out[0]
    rows = lax.all_gather(arrived, "shard", axis=0, tiled=True).reshape(-1, width)
    before_gelu = jnp.dot(rows, inner, preferred_element_type=jnp.float32)
    active = jax.nn.gelu(before_gelu).astype(jnp.bfloat16)
    partial_value = jnp.dot(active, outer, preferred_element_type=jnp.float32).reshape(
        -1, capacity, width
    )
    produced = lax.psum_scatter(
        partial_value.astype(jnp.bfloat16), "shard", scatter_dimension=0, tiled=True
    )
    returned = lax.all_to_all(produced, "expert", split_axis=0, concat_axis=0, tiled=True).reshape(
        -1, width
    )
    results = returned[slot].astype(jnp.float32).reshape(tokens_here, 2, width)
    block_out = hidden + jnp.sum(gates[:, :, None] * results, axis=1)
    gate_grad = jnp.sum(out_grad[:, None, :] * results, axis=2)
    pick_grad = gates * (gate_grad - jnp.sum(gates * gate_grad, axis=1, keepdims=True))
    logit_grad = jnp.sum(pick_grad[:, :, None] * chosen, axis=1)
    router_grad = jnp.dot(normed2.astype(jnp.float32).T, logit_grad, precision=highest)
    normed2_grad = jnp.dot(logit_grad, w_router.astype(jnp.float32).T, precision=highest)
    sent_grad = (gates[:, :, None] * out_grad[:, None, :]).reshape(-1, width).astype(jnp.bfloat16)
    padded_grad = jnp.concatenate([sent_grad, jnp.zeros((1, width), jnp.bfloat16)], axis=0)
    outgoing_grad = padded_grad[owner].reshape(experts_all, capacity, width)
    arrived_grad = lax.all_to_all(outgoing_grad, "expert", split_axis=0, concat_axis=0, tiled=True)
    rows_grad = lax.all_gather(arrived_grad, "shard", axis=0, tiled=True).reshape(-1, width)
    active_grad = jnp.einsum("rd,fd->rf", rows_grad, outer, preferred_element_type=jnp.float32)
    gelu_back = jax.vjp(jax.nn.gelu, before_gelu)[1]
    pre_grad = gelu_back(active_grad)[0].astype(jnp.bfloat16)
    outer_grad = jnp.einsum("rf,rd->fd", active, rows_grad, preferred_element_type=jnp.float32)
    inner_grad = jnp.einsum("rd,rf->df", rows, pre_grad, preferred_element_type=jnp.float32)
    row_back = jnp.einsum("rf,df->rd", pre_grad, inner, preferred_element_type=jnp.float32).reshape(
        -1, capacity, width
    )
    back_rows = lax.psum_scatter(
        row_back.astype(jnp.bfloat16), "shard", scatter_dimension=0, tiled=True
    )
    expert_in_grad = inner_grad[None]
    expert_out_grad = outer_grad[None]
    back_here = lax.all_to_all(
        back_rows, "expert", split_axis=0, concat_axis=0, tiled=True
    ).reshape(-1, width)
    normed2_grad = normed2_grad + jnp.sum(
        back_here[slot].astype(jnp.float32).reshape(tokens_here, 2, width), axis=1
    )
    hidden_back, norm2_gain_grad = norm_back(hidden, scale2, norm2_gain, normed2_grad)
    hidden_grad = out_grad + hidden_back
    attended_grad = hidden_grad.astype(jnp.bfloat16)
    attn_out_grad = jnp.einsum(
        "td,te->de", merged, attended_grad, preferred_element_type=jnp.float32
    )
    merged_grad = jnp.einsum(
        "te,de->td", attended_grad, full_attn_out, preferred_element_type=jnp.float32
    )
    merged_grad = merged_grad.astype(jnp.bfloat16).reshape(tokens_here, heads, head_dim)

    def backward_block(carry, index):
        key_grad, value_grad, diagonal_grad = carry
        start, sequence_start, offset, allowed = block_geometry(index, block_rows, seq_len, marks)
        query = lax.dynamic_slice_in_dim(queries, start, block_rows, 0)
        block_grad = lax.dynamic_slice_in_dim(merged_grad, start, block_rows, 0)
        bias_block = skewed_bias(diagonal_bias, offset, block_rows, seq_len)
        scores = block_scores(query, keys, bias_block, allowed, scale)
        shares = jnp.where(allowed[None], jnp.exp(scores - log_totals[index][:, :, None]), 0.0)
        value_part = jnp.einsum(
            "hqk,qhd->khd",
            shares.astype(jnp.bfloat16),
            block_grad,
            preferred_element_type=jnp.float32,
        )
        dots = jnp.einsum("qhd,khd->hqk", block_grad, values, preferred_element_type=jnp.float32)
        inner_sum = jnp.sum(shares * dots, axis=2, keepdims=True)
        score_grad = (shares * (dots - inner_sum)).astype(jnp.bfloat16)
        query_grad = (
            jnp.einsum("hqk,khd->qhd", score_grad, keys, preferred_element_type=jnp.float32) * scale
        )
        key_part = (
            jnp.einsum("hqk,qhd->khd", score_grad, query, preferred_element_type=jnp.float32)
            * scale
        )
        diagonal_grad = diagonal_grad + diagonal_sums(score_grad, offset, seq_len)
        key_grad = add_rows(key_grad, key_part)
        value_grad = add_rows(value_grad, value_part)
        return ((key_grad, value_grad, diagonal_grad), query_grad)

    zero_rows = jnp.zeros((tokens_here, heads, head_dim), jnp.float32)
    start_carry = (zero_rows, zero_rows, jnp.zeros((heads, 2 * seq_len), jnp.float32))
    (key_grad, value_grad, diagonal_grad), query_grads = lax.scan(
        backward_block, start_carry, jnp.arange(blocks)
    )
    rel_bias_grad = jnp.dot(diagonal_grad, bucket_table, precision=highest)
    projected_grad = jnp.concatenate(
        [
            query_grads.reshape(tokens_here, width),
            key_grad.reshape(tokens_here, width),
            value_grad.reshape(tokens_here, width),
        ],
        axis=1,
    ).astype(jnp.bfloat16)
    projection_grad = jnp.einsum(
        "td,te->de", normed, projected_grad, preferred_element_type=jnp.float32
    )
    normed_grad = jnp.einsum(
        "te,de->td", projected_grad, full_projection, preferred_element_type=jnp.float32
    )
    input_back, norm1_gain_grad = norm_back(residual_in, scale1, norm1_gain, normed_grad)
    residual_grad = hidden_grad + input_back
    projection_part, attn_out_part = (
        lax.psum_scatter(
            projection_grad.astype(jnp.bfloat16), "shard", scatter_dimension=0, tiled=True
        ).astype(jnp.float32),
        lax.psum_scatter(
            attn_out_grad.astype(jnp.bfloat16), "shard", scatter_dimension=0, tiled=True
        ).astype(jnp.float32),
    )
    projection_total, attn_out_total = lax.psum((projection_part, attn_out_part), "expert")
    gain1_total, bias_total, gain2_total, router_total = lax.psum(
        (norm1_gain_grad, rel_bias_grad, norm2_gain_grad, router_grad), ("expert", "shard")
    )
    return (
        block_out,
        residual_grad,
        gain1_total,
        projection_total,
        bias_total,
        attn_out_total,
        gain2_total,
        router_total,
        expert_in_grad,
        expert_out_grad,
    )


def solution(mesh):
    return jax.shard_map(
        per_device,
        mesh=mesh,
        in_specs=(
            P(("expert", "shard"), None),
            P(),
            P("shard", None),
            P(),
            P("shard", None),
            P(),
            P(),
            P("expert", None, "shard"),
            P("expert", "shard", None),
            P(("expert", "shard"), None),
            P(("expert", "shard"), None),
            P(("expert", "shard"), None),
        ),
        out_specs=(
            P(("expert", "shard"), None),
            P(("expert", "shard"), None),
            P(),
            P("shard", None),
            P(),
            P("shard", None),
            P(),
            P(),
            P("expert", None, "shard"),
            P("expert", "shard", None),
        ),
        check_vma=False,
    )
```

profile of v0, /device:TPU:0, one launch (start us, length us, event | category | flops | bytes accessed | tf_op | source)
XLA Modules:
  0.0 3090.6 jit_solution(6345109662171326562)
XLA Ops:
  60.5 622.7 %while.33 = (s32[]{:T(128)}, bf16[2,512,12,64]{1,3,2,0:T(8,128)(2,1)}, f32[2,12,512]{2,1,0:T(8,128)}, s32[2]{0:T(128)}, s32[1024]{0:T(1024)}, /*index=5*/s32[1,1...) while((s32[]{:T(128)}, ...), condition=%wide.region_4.5_spmd, body=%wide.region_1.4_spmd.sunk | while | flops 1669327360 | bytes 638818560 | solution.py:142
  121.3 56.5 %copy.77 = f32[2,8,512,2048]{3,1,2,0:T(8,128)} copy(f32[2,8,512,2048]{3,2,1,0:T(8,128)} %bitcast.147) | data formatting | bytes 134217728 | tf_op jit(solution)/shard_map/while
  177.8 44.3 %slice.46 = f32[12,1048064]{1,0:T(8,128)} slice(f32[12,1048576]{1,0:T(8,128)} %bitcast.148), slice={[0:12], [0:1048064]} | slice | bytes 100614144 | tf_op jit(solution)/shard_map/while/body/eval_jaxpr/slice | solution.py:49
  222.1 108.6 %reshape.591 = f32[12,512,2047]{2,1,0:T(8,128)} reshape(f32[12,1048064]{1,0:T(8,128)} %slice.46) | data formatting | bytes 100614144 | tf_op jit(solution)/shard_map/while/body/eval_jaxpr/reshape | solution.py:50
  433.6 56.5 %copy.77 = f32[2,8,512,2048]{3,1,2,0:T(8,128)} copy(f32[2,8,512,2048]{3,2,1,0:T(8,128)} %bitcast.147) | data formatting | bytes 134217728 | tf_op jit(solution)/shard_map/while
  534.4 99.5 %reshape.591 = f32[12,512,2047]{2,1,0:T(8,128)} reshape(f32[12,1048064]{1,0:T(8,128)} %slice.46) | data formatting | bytes 100614144 | tf_op jit(solution)/shard_map/while/body/eval_jaxpr/reshape | solution.py:50
  702.0 93.7 %all_to_all.20 = bf16[8,320,768]{2,1,0:T(8,128)(2,1)} all-to-all(bf16[8,320,768]{2,1,0:T(8,128)(2,1)} %bitcast.171), channel_id=1, replica_groups=mesh['expert'=8,'shard'=4] {'expert'}, dimensions={0} | all-to-all | bytes 7864320 | tf_op jit(solution)/shard_map/all_to_all | solution.py:160
  832.2 91.5 %all_to_all.21 = bf16[8,320,768]{2,1,0:T(8,128)(2,1)} all-to-all(bf16[8,320,768]{2,1,0:T(8,128)(2,1)} %bitcast.172), channel_id=1, replica_groups=mesh['expert'=8,'shard'=4] {'expert'}, dimensions={0} | all-to-all | bytes 7864320 | tf_op jit(solution)/shard_map/all_to_all | solution.py:185
  953.3 68.5 %all-gather.11.cloned.1.call-done = bf16[32,320,768]{2,1,0:T(8,128)(2,1)} async-done(((bf16[8,320,768]{2,1,0:T(8,128)(2,1)}), bf16[32,320,768]{2,1,0:T(8,128)(2,1)}) %all-gather.11.cloned.1.call-update) | async-done | bytes 15728656 | tf_op jit(solution)/shard_map/all_gather | solution.py:186
  1099.8 98.4 %reduce-scatter.7.cloned.1.call-done = bf16[8,320,768]{2,1,0:T(8,128)(2,1)} async-done(((bf16[32,320,768]{2,1,0:T(8,128)(2,1)}), bf16[8,320,768]{2,1,0:T(8,128)(2,1)}) %reduce-scatter.7.cloned.1.call-update) | async-done | bytes 3932176 | tf_op jit(solution)/shard_map/reduce_scatter | solution.py:195
  1203.8 116.8 %reduce-scatter.5.cloned.1.call-done = bf16[8,320,768]{2,1,0:T(8,128)(2,1)} async-done(((bf16[32,320,768]{2,1,0:T(8,128)(2,1)}), bf16[8,320,768]{2,1,0:T(8,128)(2,1)}) %reduce-scatter.5.cloned.1.call-update) | async-done | bytes 3932176 | tf_op jit(solution)/shard_map/reduce_scatter | solution.py:169
  1338.9 74.9 %all-to-all-done.1 = bf16[8,320,768]{2,1,0:T(8,128)(2,1)} async-done(((bf16[8,320,768]{2,1,0:T(8,128)(2,1)}), bf16[8,320,768]{2,1,0:T(8,128)(2,1)}, u32[]{:S(2)}, u32[]{:S(2)}) %all-to-all-start.1) | async-done | bytes 3932192 | tf_op jit(solution)/shard_map/all_to_all | solution.py:172
  1491.1 1381.1 %while.34 = (s32[]{:T(128)}, f32[1024,12,64]{0,2,1:T(8,128)}, f32[1024,12,64]{0,2,1:T(8,128)}, f32[12,2048]{1,0:T(8,128)}, bf16[2,512,12,64]{1,3,2,0:T(8,128)(2,...) while((s32[]{:T(128)}, f32[1024,12,64]{0,2,1:T(8,128)}, ...), condition=%wide.region_24.25_spmd.clone, body=%wide.region_21.24_spmd.clone.sunk | while | flops 4127345152 | bytes 1123735936 | solution.py:248
  1566.8 56.5 %copy.78 = f32[2,8,512,2048]{3,1,2,0:T(8,128)} copy(f32[2,8,512,2048]{3,2,1,0:T(8,128)} %bitcast.161) | data formatting | bytes 134217728 | tf_op jit(solution)/shard_map/while
  1667.6 99.4 %reshape.592 = f32[12,512,2047]{2,1,0:T(8,128)} reshape(f32[12,1048064]{1,0:T(8,128)} %slice.48) | data formatting | bytes 100614144 | tf_op jit(solution)/shard_map/while/body/eval_jaxpr/reshape | solution.py:50
  1838.6 124.1 %dynamic_update_slice.38 = bf16[12,512,2047]{2,1,0:T(8,128)(2,1)} dynamic-update-slice(bf16[12,512,2047]{2,1,0:T(8,128)(2,1)} %broadcast.533, bf16[12,512,1024]{2,1,0:T(8,128)(2,1)} %multiply_convert_fusion.8, s32[]{:T(128)} %constant.229.clone.1..sunk.1, s32[]{:T(128)} %constant.229.clone.1..sunk.1, s32[]{:T(128)S(6)} %select_n.134) | dynamic-update-slice | bytes 25165828 | tf_op jit(solution)/shard_map/while/body/eval_jaxpr/dynamic_update_slice | solution.py:58
  1980.9 89.5 %reshape.593 = bf16[12,1048064]{1,0:T(8,128)(2,1)} reshape(bf16[12,512,2047]{2,1,0:T(8,128)(2,1)} %dynamic_update_slice.38) | data formatting | bytes 50307072 | tf_op jit(solution)/shard_map/while/body/eval_jaxpr/reshape | solution.py:59
  2103.0 56.4 %copy.79 = f32[2,8,512,2048]{3,2,1,0:T(8,128)} copy(f32[2,8,512,2048]{3,1,2,0:T(8,128)} %bitcast.164) | data formatting | bytes 134217728 | tf_op jit(solution)/shard_map/while
  2253.2 56.5 %copy.78 = f32[2,8,512,2048]{3,1,2,0:T(8,128)} copy(f32[2,8,512,2048]{3,2,1,0:T(8,128)} %bitcast.161) | data formatting | bytes 134217728 | tf_op jit(solution)/shard_map/while
  2354.0 99.4 %reshape.592 = f32[12,512,2047]{2,1,0:T(8,128)} reshape(f32[12,1048064]{1,0:T(8,128)} %slice.48) | data formatting | bytes 100614144 | tf_op jit(solution)/shard_map/while/body/eval_jaxpr/reshape | solution.py:50
  2526.0 125.1 %dynamic_update_slice.38 = bf16[12,512,2047]{2,1,0:T(8,128)(2,1)} dynamic-update-slice(bf16[12,512,2047]{2,1,0:T(8,128)(2,1)} %broadcast.533, bf16[12,512,1024]{2,1,0:T(8,128)(2,1)} %multiply_convert_fusion.8, s32[]{:T(128)} %constant.229.clone.1..sunk.1, s32[]{:T(128)} %constant.229.clone.1..sunk.1, s32[]{:T(128)S(6)} %select_n.134) | dynamic-update-slice | bytes 25165828 | tf_op jit(solution)/shard_map/while/body/eval_jaxpr/dynamic_update_slice | solution.py:58
  2670.2 89.5 %reshape.593 = bf16[12,1048064]{1,0:T(8,128)(2,1)} reshape(bf16[12,512,2047]{2,1,0:T(8,128)(2,1)} %dynamic_update_slice.38) | data formatting | bytes 50307072 | tf_op jit(solution)/shard_map/while/body/eval_jaxpr/reshape | solution.py:59
  2792.3 56.4 %copy.79 = f32[2,8,512,2048]{3,2,1,0:T(8,128)} copy(f32[2,8,512,2048]{3,1,2,0:T(8,128)} %bitcast.164) | data formatting | bytes 134217728 | tf_op jit(solution)/shard_map/while
  2981.8 101.8 %all-reduce.6 = (f32[192,2304]{1,0:T(8,128)}, f32[192,768]{1,0:T(8,128)}) all-reduce(bf16[192,2304]{1,0:T(8,128)(2,1)} %reduce-scatter.9.cloned.1.call-done, bf16[192,768]{1,0:T(8,128)(2,1)} %reduce-scatter.11.cloned.1.call-done), channel_id=1, replica_groups=mesh['expert'=8,'shard'=4] {'expert'}, use_global_device_ids=true, to_apply=%region_29.30 | all-reduce | flops 589824 | bytes 3538944 | tf_op jit(solution)/shard_map/psum | solution.py:276
  (336 shorter events, 1190.4 us)
Async XLA Ops:
  7.2 916.7 %copy-start = (bf16[1,768,768]{2,1,0:T(8,128)(2,1)S(1)}, bf16[1,768,768]{2,1,0:T(8,128)(2,1)}, u32[]{:S(2)}) copy-start(bf16[1,768,768]{2,1,0:T(8,128)(2,1)} %param.23) | copy-start | bytes 3538948
  7.2 35.9 %all-gather.5.cloned.1.call-start = ((), (), s32[]{:S(2)}) async-start(), calls=%async_computation.8 | async-start | bytes 4423680 | tf_op jit(solution)/shard_map/all_gather | solution.py:113
  7.9 678.8 %all-gather.7.cloned.1.call-start = ((), (), s32[]{:S(2)}) async-start(), calls=%async_computation.9 | async-start | bytes 1474560 | tf_op jit(solution)/shard_map/all_gather | solution.py:114
  8.7 915.1 %all-gather.9.cloned.1.call-start = ((), (), s32[]{:S(2)}) async-start(), calls=%async_computation.10 | async-start | bytes 19660800 | tf_op jit(solution)/shard_map/all_gather | solution.py:163
  222.1 108.6 %copy-start.6 = (bf16[1024,12,64]{0,2,1:T(8,128)(2,1)S(1)}, bf16[1024,12,64]{0,2,1:T(8,128)(2,1)}, u32[]{:S(2)}) copy-start(bf16[1024,12,64]{0,2,1:T(8,128)(2,1)} %get-tuple-element.669) | copy-start | bytes 4718596 | tf_op jit(solution)/shard_map/while
  222.1 108.6 %copy-start.8 = (pred[512,1024]{1,0:T(8,128)(4,1)S(1)}, pred[512,1024]{1,0:T(8,128)(4,1)}, u32[]{:S(2)}) copy-start(pred[512,1024]{1,0:T(8,128)(4,1)} %fusion.121) | copy-start | bytes 1572868 | tf_op jit(solution)/shard_map/while
  534.4 99.5 %copy-start.6 = (bf16[1024,12,64]{0,2,1:T(8,128)(2,1)S(1)}, bf16[1024,12,64]{0,2,1:T(8,128)(2,1)}, u32[]{:S(2)}) copy-start(bf16[1024,12,64]{0,2,1:T(8,128)(2,1)} %get-tuple-element.669) | copy-start | bytes 4718596 | tf_op jit(solution)/shard_map/while
  534.4 99.5 %copy-start.8 = (pred[512,1024]{1,0:T(8,128)(4,1)S(1)}, pred[512,1024]{1,0:T(8,128)(4,1)}, u32[]{:S(2)}) copy-start(pred[512,1024]{1,0:T(8,128)(4,1)} %fusion.121) | copy-start | bytes 1572868 | tf_op jit(solution)/shard_map/while
  795.7 226.1 %all-gather.11.cloned.1.call-start = ((), (), s32[]{:S(2)}) async-start(), calls=%async_computation.12 | async-start | bytes 19660800 | tf_op jit(solution)/shard_map/all_gather | solution.py:186
  923.8 274.5 %reduce-scatter.7.cloned.1.call-start = ((), (), s32[]{:S(2)}) async-start(), calls=%async_computation.13 | async-start | bytes 19660800 | tf_op jit(solution)/shard_map/reduce_scatter | solution.py:195
  923.8 97.9 %copy-start.68 = (bf16[1,768,768]{2,1,0:T(8,128)(2,1)S(1)}, bf16[1,768,768]{2,1,0:T(8,128)(2,1)}, u32[]{:S(2)}) copy-start(bf16[1,768,768]{2,1,0:T(8,128)(2,1)} %param.24) | copy-start | bytes 3538948
  1078.2 242.3 %reduce-scatter.5.cloned.1.call-start = ((), (), s32[]{:S(2)}) async-start(), calls=%async_computation.11 | async-start | bytes 19660800 | tf_op jit(solution)/shard_map/reduce_scatter | solution.py:169
  1198.2 122.3 %all-to-all-start.3 = ((bf16[8,320,768]{2,1,0:T(8,128)(2,1)}), bf16[8,320,768]{2,1,0:T(8,128)(2,1)}, u32[]{:S(2)}, u32[]{:S(2)}) async-start(bf16[8,320,768]{2,1,0:T(8,128)(2,1)} %reduce-scatter.7.cloned.1.call-done), calls=%async_computation.5 | async-start | bytes 7864320 | tf_op jit(solution)/shard_map/all_to_all | solution.py:200
  1203.7 122.4 %copy-start.59 = (s32[2048,1]{0,1:T(1,128)S(1)}, s32[2048,1]{0,1:T(1,128)}, u32[]{:S(2)}) copy-start(s32[2048,1]{0,1:T(1,128)} %copy-done.58) | copy-start | bytes 24580
  1320.6 93.2 %all-to-all-start.1 = ((bf16[8,320,768]{2,1,0:T(8,128)(2,1)}), bf16[8,320,768]{2,1,0:T(8,128)(2,1)}, u32[]{:S(2)}, u32[]{:S(2)}) async-start(bf16[8,320,768]{2,1,0:T(8,128)(2,1)} %reduce-scatter.5.cloned.1.call-done), calls=%async_computation.2 | async-start | bytes 7864320 | tf_op jit(solution)/shard_map/all_to_all | solution.py:172
  1326.1 1655.7 %reduce-scatter.11.cloned.1.call-start = ((), (), s32[]{:S(2)}) async-start(), calls=%async_computation.15 | async-start | bytes 1474560 | tf_op jit(solution)/shard_map/reduce_scatter | solution.py:272
  1484.3 1497.5 %reduce-scatter.9.cloned.1.call-start = ((), (), s32[]{:S(2)}) async-start(), calls=%async_computation.14 | async-start | bytes 4423680 | tf_op jit(solution)/shard_map/reduce_scatter | solution.py:269
  1667.6 99.5 %copy-start.7 = (bf16[1024,12,64]{0,2,1:T(8,128)(2,1)S(1)}, bf16[1024,12,64]{0,2,1:T(8,128)(2,1)}, u32[]{:S(2)}) copy-start(bf16[1024,12,64]{0,2,1:T(8,128)(2,1)} %get-tuple-element.740) | copy-start | bytes 4718596 | tf_op jit(solution)/shard_map/while
  1667.6 99.5 %copy-start.21 = (pred[512,1024]{1,0:T(8,128)(4,1)S(1)}, pred[512,1024]{1,0:T(8,128)(4,1)}, u32[]{:S(2)}) copy-start(pred[512,1024]{1,0:T(8,128)(4,1)} %fusion.134) | copy-start | bytes 1572868 | tf_op jit(solution)/shard_map/while
  1667.6 99.5 %copy-start.39 = (f32[12,512]{1,0:T(8,128)S(1)}, f32[12,512]{1,0:T(8,128)}, u32[]{:S(2)}) copy-start(f32[12,512]{1,0:T(8,128)} %dynamic-slice_bitcast_fusion.2) | copy-start | bytes 73732 | tf_op jit(solution)/shard_map/while
  2354.0 99.5 %copy-start.7 = (bf16[1024,12,64]{0,2,1:T(8,128)(2,1)S(1)}, bf16[1024,12,64]{0,2,1:T(8,128)(2,1)}, u32[]{:S(2)}) copy-start(bf16[1024,12,64]{0,2,1:T(8,128)(2,1)} %get-tuple-element.740) | copy-start | bytes 4718596 | tf_op jit(solution)/shard_map/while
  2354.0 99.5 %copy-start.21 = (pred[512,1024]{1,0:T(8,128)(4,1)S(1)}, pred[512,1024]{1,0:T(8,128)(4,1)}, u32[]{:S(2)}) copy-start(pred[512,1024]{1,0:T(8,128)(4,1)} %fusion.134) | copy-start | bytes 1572868 | tf_op jit(solution)/shard_map/while
  2354.0 99.5 %copy-start.39 = (f32[12,512]{1,0:T(8,128)S(1)}, f32[12,512]{1,0:T(8,128)}, u32[]{:S(2)}) copy-start(f32[12,512]{1,0:T(8,128)} %dynamic-slice_bitcast_fusion.2) | copy-start | bytes 73732 | tf_op jit(solution)/shard_map/while
  2975.4 108.2 %copy-start.1 = (bf16[1,768,768]{2,1,0:T(8,128)(2,1)S(1)}, bf16[1,768,768]{2,1,0:T(8,128)(2,1)}, u32[]{:S(2)}) copy-start(bf16[1,768,768]{2,1,0:T(8,128)(2,1)} %param.23) | copy-start | bytes 3538948
  (71 other events, 805.4 us)
Sparse Core Ops, SparseCore 0:
  9.6 33.4 all-gather.4
  44.6 17.4 all-gather.6
  795.8 98.0 all-gather.8
  923.9 97.8 all-gather.10
  1078.3 119.8 reduce-scatter.6
  1200.7 119.8 reduce-scatter.4
  1484.4 23.8 reduce-scatter.10
  2889.1 38.5 reduce-scatter.8
where the time goes:
time: 3110 us; the launch traced here: 3090 us
  local copies, waits for them, and re-layouts  1720 us (55%)
  matrix products  394 us (13%)
  waiting for transfers between devices  380 us (12%)
  blocking collectives  326 us (10%)
  other arithmetic  223 us (7%)
    while x70, local copies, waits for them, and re-layouts  499 us
    reshape x4, local copies, waits for them, and re-layouts, skewed_bias(): sheared = tiled.reshape(heads, block_rows, wide - 1)  407 us
    dynamic_update_slice x2, local copies, waits for them, and re-layouts, diagonal_sums(): lax.dynamic_update_slice_in_dim(placed, score_grad, seq_len - 1 - offset, 2)  249 us
    reshape x2, local copies, waits for them, and re-layouts, diagonal_sums(): flat = placed.reshape(heads, block_rows * (wide - 1))  179 us
    slice x4, local copies, waits for them, and re-layouts, skewed_bias(): jnp.tile(diagonal_bias, (1, block_rows))[:, :block_rows * (wide - 1)]  177 us
    reduce_scatter x1, waiting for transfers between devices, per_device(): lax.psum_scatter(partial_value.astype(jnp.bfloat16), 'shard', scatter_dim...  117 us
    psum x1, blocking collectives, per_device(): lax.psum((projection_part, attn_out_part), 'expert')  102 us
    reduce_scatter x1, waiting for transfers between devices, per_device(): lax.psum_scatter(row_back.astype(jnp.bfloat16), 'shard', scatter_dimensio...  98.4 us
  transfers between devices with their start and end apart: 10, of which 5 were waited for; matrix products, arithmetic and copies ran while one was open for 71% of the time, Pallas kernels for 0%

commit v1 on v0

v1 whole, which is shorter than its diff:
```python
import functools

import jax
import jax.numpy as jnp
import numpy as np
from jax import lax
from jax.experimental import pallas as pl
from jax.experimental.pallas import tpu as pltpu
from jax.sharding import PartitionSpec as P

bucket_borders = (19, 21, 24, 27, 31, 35, 40, 46, 52, 59, 67, 77, 87, 99, 113)
longest = 512
tile = 256
span = 3 * tile
lanes = 128
masked = -1e30
f32 = jnp.float32
bf16 = jnp.bfloat16


def one_hot_buckets(distance, buckets):
    distance = np.clip(distance, 0, None)
    beyond = sum((distance >= border).astype(np.int32) for border in bucket_borders)
    bucket = np.where(distance < 16, distance, 16 + beyond)
    return (bucket[:, None] == np.arange(buckets)[None, :]).astype(np.float32)


def bias_tables(buckets):
    lane = np.arange(span)
    rows = np.where(lane < 2 * tile, tile - lane, tile + span - lane)
    turned = np.where(lane < tile, tile + lane, tile + lane - span)
    return (one_hot_buckets(rows, buckets), one_hot_buckets(turned, buckets))


def key_start(first):
    return max(0, first - longest) // tile * tile


def dot_nt(a, b):
    return lax.dot_general(a, b, (((1,), (1,)), ((), ())), preferred_element_type=f32)


def dot_tn(a, b):
    return lax.dot_general(a, b, (((0,), (0,)), ((), ())), preferred_element_type=f32)


def dot_nn(a, b):
    return lax.dot_general(a, b, (((1,), (0,)), ((), ())), preferred_element_type=f32)


def attend_forward_pair(
    head_dim, pair, q_ref, k_ref, v_ref, base_ref, out_ref, log_ref, mask_ref
):
    seq_len = q_ref.shape[0]
    scale = head_dim ** (-0.5)
    per_pair = lanes // head_dim
    lane = lax.broadcasted_iota(jnp.int32, (tile, lanes), 1)
    tables = []
    for head in range(per_pair):
        wide = jnp.broadcast_to(base_ref[head : head + 1, :], (tile, span))
        tables.append(pltpu.roll(wide, 0, 1, stride=1, stride_axis=0))
    for first in range(0, seq_len, tile):
        start = key_start(first)
        merged = jnp.zeros((tile, lanes), f32)
        logs = log_ref[first : first + tile, :]
        for head in range(per_pair):
            inside = (lane >= head * head_dim) & (lane < (head + 1) * head_dim)
            query = jnp.where(inside, q_ref[first : first + tile, :] * scale, 0.0).astype(bf16)
            pieces = []
            for begin in range(start, first + tile, tile):
                piece = dot_nt(query, k_ref[begin : begin + tile, :])
                back = (first - begin) // tile
                if back == 0:
                    piece = piece + tables[head][:, tile : 2 * tile]
                elif back == 1:
                    piece = piece + tables[head][:, :tile]
                else:
                    piece = piece + base_ref[head : head + 1, :1]
                place = begin - start
                pieces.append(piece + mask_ref[first : first + tile, place : place + tile])
            peak = functools.reduce(jnp.maximum, pieces)
            peak = jnp.max(peak, axis=1, keepdims=True)
            weights = [jnp.exp(piece - peak) for piece in pieces]
            total = jnp.sum(functools.reduce(jnp.add, weights), axis=1, keepdims=True)
            mixed = jnp.zeros((tile, lanes), f32)
            for index, weight in enumerate(weights):
                begin = start + index * tile
                mixed = mixed + dot_nn(weight.astype(bf16), v_ref[begin : begin + tile, :])
            merged = jnp.where(inside, mixed * (1.0 / total), merged)
            logs = jnp.where(lane == pair * per_pair + head, peak + jnp.log(total), logs)
        out_ref[first : first + tile, :] = merged.astype(bf16)
        log_ref[first : first + tile, :] = logs


def attend_backward_pair(
    head_dim,
    pair,
    q_ref,
    k_ref,
    v_ref,
    grad_ref,
    base_ref,
    dq_ref,
    dk_ref,
    dv_ref,
    bias_ref,
    mask_ref,
    log_turned,
    dk_total,
    dv_total,
    diagonal,
):
    seq_len = q_ref.shape[0]
    scale = head_dim ** (-0.5)
    per_pair = lanes // head_dim
    firsts = range(0, seq_len, tile)
    dk_total[...] = jnp.zeros_like(dk_total)
    dv_total[...] = jnp.zeros_like(dv_total)
    lane = lax.broadcasted_iota(jnp.int32, (tile, lanes), 1)
    tables = []
    for head in range(per_pair):
        wide = jnp.broadcast_to(base_ref[head : head + 1, :], (2 * tile, span))
        tables.append(pltpu.roll(wide, 0, 1, stride=1, stride_axis=0)[:, :tile])
    diagonal[...] = jnp.zeros_like(diagonal)
    far = [jnp.zeros((1, tile), f32) for _ in range(per_pair)]
    for first in firsts:
        start = key_start(first)
        query_grad = jnp.zeros((tile, lanes), f32)
        for head in range(per_pair):
            inside = (lane >= head * head_dim) & (lane < (head + 1) * head_dim)

            def own(values):
                return jnp.where(inside, values, 0.0).astype(bf16)

            query = own(q_ref[first : first + tile, :] * scale)
            grad = own(grad_ref[first : first + tile, :])
            row = log_turned[pl.ds(pair * per_pair + head, 1), first : first + tile]
            begins = range(start, first + tile, tile)
            shares, dots = [], []
            inner = jnp.zeros((1, tile), f32)
            for begin in begins:
                piece = dot_nt(k_ref[begin : begin + tile, :], query)
                back = (first - begin) // tile
                if back == 0:
                    piece = piece + tables[head][tile:, :]
                elif back == 1:
                    piece = piece + tables[head][:tile, :]
                else:
                    piece = piece + base_ref[head : head + 1, :1]
                place = begin - start
                piece = piece + mask_ref[place : place + tile, first : first + tile]
                share = jnp.exp(piece - row)
                dot = dot_nt(v_ref[begin : begin + tile, :], grad)
                inner = inner + jnp.sum(share * dot, axis=0, keepdims=True)
                dv_total[begin : begin + tile, :] += dot_nn(share.astype(bf16), grad)
                shares.append(share)
                dots.append(dot)
            for begin, share, dot in zip(begins, shares, dots):
                back = (first - begin) // tile
                score_grad = share * (dot - inner)
                if back < 2:
                    top = (1 - back) * tile
                    diagonal[head, top : top + tile, :tile] += score_grad
                else:
                    far[head] = far[head] + jnp.sum(score_grad, axis=0, keepdims=True)
                score_grad = score_grad.astype(bf16)
                dk_total[begin : begin + tile, :] += dot_nn(score_grad, query)
                query_grad = query_grad + dot_tn(
                    score_grad, own(k_ref[begin : begin + tile, :] * scale)
                )
        dq_ref[first : first + tile, :] = query_grad.astype(bf16)
    dk_ref[...] = dk_total[...].astype(bf16)
    dv_ref[...] = dv_total[...].astype(bf16)
    for head in range(per_pair):
        grouped = diagonal[head, :8, :]
        for top in range(8, 2 * tile, 8):
            grouped = grouped + pltpu.roll(diagonal[head, top : top + 8, :], span - top, 1)
        sums = grouped[:1, :]
        for row in range(1, 8):
            sums = sums + pltpu.roll(grouped[row : row + 1, :], span - row, 1)
        bias_ref[head : head + 1, :tile] = sums[:, :tile] + far[head]
        bias_ref[head : head + 1, tile:] = sums[:, tile:]


hidden_tile = 768
block_count = 4
epsilon = 1e-06
mesh_ids = pl.DeviceIdType.MESH


def gelu_parts(values):
    factor = 0.7978845608028654
    squares = values * values
    turned = jnp.tanh(values * (factor + (factor * 0.044715) * squares))
    share = 0.5 + 0.5 * turned
    active = values * share
    inside = 2.0 * factor + (6.0 * factor * 0.044715) * squares
    return (active, share + active * ((1.0 - share) * inside))


def turned_row(row):
    return jnp.broadcast_to(row.astype(f32), (lanes, row.shape[1])).T


def split_digits(row):
    places = lax.broadcasted_iota(jnp.int32, (8, row.shape[1]), 0)
    digits = jnp.zeros(places.shape, f32)
    for place in range(3):
        digit = row.astype(bf16).astype(f32)
        digits = jnp.where(places == place, digit, digits)
        row = row - digit
    return digits.astype(bf16)


def paired(place, step, members):
    partner, bit = 0, 1
    while bit < members:
        ours, theirs = place // bit % 2, step // bit % 2
        partner = partner + bit * (ours + theirs - 2 * ours * theirs)
        bit = 2 * bit
    return partner


def group_place(members, shards):
    expert, shard = lax.axis_index("expert"), lax.axis_index("shard")
    half, side = members // 2, shards // 2

    def device_of(member):
        return {
            "expert": expert // half * half + lax.rem(member, half),
            "shard": member // half * side + lax.rem(shard, side),
        }

    return shard // side * half + lax.rem(expert, half), device_of


def add_remote(source, target, send, arrive, device):
    return pltpu.make_async_remote_copy(
        src_ref=source,
        dst_ref=target,
        send_sem=send,
        recv_sem=arrive,
        device_id=device,
        device_id_type=mesh_ids,
    )


def expert_kernel(
    shards,
    sent_ref,
    gates_ref,
    grads_ref,
    inner_ref,
    outer_ref,
    gated_out,
    back_out,
    gates_out,
    active_out,
    pre_out,
    inner_mine,
    outer_mine,
    outer_given,
    inner_crossed,
    inner_distant,
    rows,
    grads_held,
    scaled,
    actives,
    pres,
    gates_in,
    gates_back,
    value_total,
    row_total,
    inner_held,
    outer_held,
    turned,
    near_in,
    send_sems,
    arrive_sems,
    back_sems,
    returned_sems,
    gate_send,
    gate_arrive,
    digit_sems,
    digit_arrive,
    load_sems,
    weight_sems,
    active_sems,
    pre_sems,
    tile_sems,
    keep_sems,
    near_send,
    near_arrive,
    across_sems,
    distant_sems,
):
    members, capacity, _ = sent_ref.shape
    blocks, block, width = rows.shape
    units = actives.shape[2]
    quarters = actives.shape[1] // block
    block_steps = members // blocks
    me, device_of = group_place(members, shards)
    shard = lax.axis_index("shard")
    side = shards // 2
    low, turn = lax.rem(shard, side), shard // side
    far_low = lax.rem(low + 1, side)
    across = {"shard": lax.rem(shard + side, shards)}
    near = {"shard": turn * side + far_low}
    expert, half = lax.axis_index("expert"), members // 2
    native_here = expert // half == turn
    distant = {"expert": lax.rem(expert + half, members)}

    def source(step):
        return paired(me, step, members)

    def device(step):
        return device_of(source(step))

    def place_of(ref, step):
        start = pl.multiple_of(lax.rem(step, block_steps) * capacity, 16)
        return ref.at[step // block_steps, pl.ds(start, capacity)]

    def sending(step):
        return add_remote(
            sent_ref.at[source(step)],
            place_of(rows, step),
            send_sems.at[step],
            arrive_sems.at[step],
            device(step),
        )

    def sending_gates(step):
        return add_remote(
            gates_ref.at[source(step)],
            gates_in.at[step],
            gate_send.at[step],
            gate_arrive.at[step],
            device(step),
        )

    def returning(step):
        return add_remote(
            place_of(rows, step),
            back_out.at[me],
            back_sems.at[step],
            returned_sems.at[step],
            device(step),
        )

    def returning_gates(step):
        return add_remote(
            gates_back.at[step],
            gates_out.at[me],
            digit_sems.at[step],
            digit_arrive.at[step],
            device(step),
        )

    def loading(step):
        return pltpu.make_async_copy(
            grads_ref.at[source(step)], place_of(grads_held, step), load_sems.at[step]
        )

    def giving(step):
        return pltpu.make_async_copy(
            place_of(grads_held, step), gated_out.at[source(step)], load_sems.at[step]
        )

    def keeping(index, slot):
        return (
            pltpu.make_async_copy(actives.at[slot], active_out.at[index], active_sems.at[slot]),
            pltpu.make_async_copy(pres.at[slot], pre_out.at[index], pre_sems.at[slot]),
        )

    own_rows = pltpu.make_async_copy(sent_ref.at[me], place_of(rows, 0), arrive_sems.at[0])
    own_back = pltpu.make_async_copy(place_of(rows, 0), back_out.at[me], back_sems.at[0])
    own_digits = pltpu.make_async_copy(gates_back.at[0], gates_out.at[me], digit_sems.at[0])
    own_gates = pltpu.make_async_copy(gates_ref.at[me], gates_in.at[0], gate_arrive.at[0])
    weight_loads = (
        pltpu.make_async_copy(inner_ref, inner_held, weight_sems.at[0]),
        pltpu.make_async_copy(outer_ref, outer_held, weight_sems.at[1]),
    )
    barrier = pltpu.get_barrier_semaphore()
    for partner in (near, distant):
        pl.semaphore_signal(barrier, inc=1, device_id=partner, device_id_type=mesh_ids)

    @pl.loop(1, members)
    def _(step):
        pl.semaphore_signal(barrier, inc=1, device_id=device(step), device_id_type=mesh_ids)

    own_rows.start()
    own_gates.start()
    for copy in weight_loads:
        copy.start()

    @pl.loop(0, members)
    def _(step):
        loading(step).start()

    pl.semaphore_wait(barrier, members + 1)

    @pl.loop(1, members)
    def _(step):
        sending_gates(step).start()
        sending(step).start()

    for copy in weight_loads:
        copy.wait()
    own_rows.wait()
    own_gates.wait()

    @pl.loop(0, blocks)
    def _(index):
        slot = lax.rem(index, 2)

        @pl.loop(0, block_steps)
        def _(place):
            step = index * block_steps + place

            @pl.when(step > 0)
            def _():
                sending_gates(step).wait_recv()
                sending(step).wait_recv()

            loading(step).wait()

        @pl.when(index > 1)
        def _():
            for copy in keeping(index - 2, slot):
                copy.wait()

        gates = jnp.concatenate(
            [
                turned_row(gates_in[index * block_steps + place, :1, :])[:capacity, :1]
                for place in range(block_steps)
            ],
            axis=0,
        )
        scaled[...] = (gates * grads_held[index].astype(f32)).astype(bf16)
        held_columns = pl.ds(pl.multiple_of(index * block, lanes), block)
        turned[0, :, held_columns] = rows[index].T
        turned[1, :, held_columns] = scaled[...].T
        value_total[...] = jnp.zeros_like(value_total)
        row_total[...] = jnp.zeros_like(row_total)

        def units_of(part):
            return pl.ds(pl.multiple_of(part * units, units), units)

        def block_of(part):
            return pl.ds(pl.multiple_of(part * block, 16), block)

        def begin_part(part):
            active, slope = gelu_parts(dot_nn(rows[index], inner_held[:, units_of(part)]))
            actives[slot, block_of(part), :] = active.astype(bf16)
            pre = dot_nt(scaled[...], outer_held[units_of(part), :]) * slope
            pres[slot, block_of(part), :] = pre.astype(bf16)

        def end_part(part):
            value_total[...] += dot_nn(actives[slot, block_of(part), :], outer_held[units_of(part), :])
            row_total[...] += dot_nt(pres[slot, block_of(part), :], inner_held[:, units_of(part)])

        begin_part(0)

        @pl.loop(1, quarters)
        def _(part):
            end_part(part - 1)
            begin_part(part)

        end_part(quarters - 1)
        for copy in keeping(index, slot):
            copy.start()
        produced = value_total[...]
        rows[index] = row_total[...].astype(bf16)
        rest = jnp.sum(grads_held[index].astype(f32) * produced, axis=1, keepdims=True)
        grads_held[index] = (gates * produced).astype(bf16)
        spare = gates_back.shape[2] - capacity
        for place in range(block_steps):
            wide = jnp.broadcast_to(
                rest[place * capacity : (place + 1) * capacity, :], (capacity, lanes)
            )
            wide = jnp.concatenate([wide, jnp.zeros((spare, lanes), f32)], axis=0)
            gates_back[index * block_steps + place] = wide.T[:8, :]

        @pl.loop(0, block_steps)
        def _(place):
            step = index * block_steps + place
            giving(step).start()

            @pl.when(step > 0)
            def _():
                returning(step).start()
                returning_gates(step).start()

            @pl.when(step == 0)
            def _():
                own_back.start()
                own_digits.start()

    held_parts = (inner_held, outer_held)
    targets = {(0, 3): inner_mine, (1, 3): outer_mine, (1, 2): outer_given}
    places = (2 * far_low, 2 * far_low + 1, 2 * low + 1, 2 * low)
    order = [(matrix, position) for matrix in range(2) for position in range(4)]
    buffers = (actives.at[0], pres.at[0], actives.at[1], pres.at[1])

    def part_of(matrix, position):
        if matrix == 0:
            return inner_held.at[:, position * units : (position + 1) * units]
        return outer_held.at[position * width : (position + 1) * width, :]

    def tile_loads(count):
        matrix, position = order[count]
        kept = (pre_out, active_out)[matrix]
        start = pl.multiple_of(places[position] * block, 16)
        return [
            pltpu.make_async_copy(
                kept.at[index, pl.ds(start, block), :],
                buffers[count % 4].at[index * block : (index + 1) * block, :],
                tile_sems.at[count % 4, index],
            )
            for index in range(blocks)
        ]

    def near_copy(matrix, position):
        return add_remote(
            part_of(matrix, position),
            near_in.at[matrix, position],
            near_send.at[matrix, position],
            near_arrive.at[matrix, position],
            near,
        )

    lines_each = width // 4

    def lines_of(index):
        return slice(index * lines_each, (index + 1) * lines_each)

    def across_copy(index):
        return add_remote(
            part_of(0, 2).at[lines_of(index), :],
            inner_crossed.at[lines_of(index), :],
            across_sems.at[0, index],
            across_sems.at[1, index],
            across,
        )

    def distant_copy(index, source):
        return add_remote(
            source.at[lines_of(index), :],
            inner_distant.at[lines_of(index), :],
            distant_sems.at[0, index],
            distant_sems.at[1, index],
            distant,
        )

    def pass_on(index):
        @pl.when(native_here)
        def _():
            across_copy(index).wait_recv()
            distant_copy(index, inner_crossed).start()

    def keep_copy(matrix, position):
        index = {(0, 3): 0, (1, 3): 1, (1, 2): 2}[matrix, position]
        return pltpu.make_async_copy(
            part_of(matrix, position), targets[matrix, position], keep_sems.at[index]
        )

    for index in range(blocks - 2, blocks):
        for copy in keeping(index, index % 2):
            copy.wait()
    for count in range(4):
        for copy in tile_loads(count):
            copy.start()
    for count, (matrix, position) in enumerate(order):
        for copy in tile_loads(count):
            copy.wait()
        target = part_of(matrix, position)

        @pl.loop(0, units // tile)
        def _(part):
            columns = pl.ds(pl.multiple_of(part * tile, tile), tile)
            sums = dot_nn(turned[matrix], buffers[count % 4][:, columns])
            target[:, columns] = sums.astype(bf16)

        if count + 4 < len(order):
            for copy in tile_loads(count + 4):
                copy.start()
        if position < 2:
            near_copy(matrix, position).start()
        else:
            other = 3 - position
            near_copy(matrix, other).wait_recv()

            @pl.loop(0, width // tile)
            def _(part):
                lines = pl.ds(pl.multiple_of(part * tile, tile), tile)
                sums = target[lines, :].astype(f32) + near_in[matrix, other, lines, :].astype(f32)
                target[lines, :] = sums.astype(bf16)

            if (matrix, position) == (0, 2):
                for index in range(4):
                    across_copy(index).start()
            else:
                keep_copy(matrix, position).start()
            if (matrix, position) == (0, 3):

                @pl.when(jnp.logical_not(native_here))
                def _():
                    for index in range(2):
                        distant_copy(index, part_of(0, 3)).start()

        if count in (4, 6):
            pass_on((count - 4) // 2)

    own_back.wait()
    own_digits.wait()

    @pl.loop(1, members)
    def _(step):
        sending_gates(step).wait_send()
        sending(step).wait_send()
        returning(step).wait()
        returning_gates(step).wait()

    @pl.loop(0, members)
    def _(step):
        giving(step).wait()

    for matrix, position in targets:
        keep_copy(matrix, position).wait()
    @pl.when(jnp.logical_not(native_here))
    def _():
        for index in range(2):
            across_copy(index).wait_recv()

    for index in range(4):
        across_copy(index).wait_send()
        if index < 2:
            distant_copy(index, inner_crossed).wait()
        else:
            across_copy(index).wait_recv()
    for matrix in range(2):
        for position in range(2):
            near_copy(matrix, position).wait_send()


def run_experts(sent, gates, grads, inner, outer, shards):
    members, capacity, width = sent.shape
    hidden_units = inner.shape[1]
    units = hidden_units // shards
    blocks = block_count
    block = members // blocks * capacity
    anywhere = pl.BlockSpec(memory_space=pl.ANY)
    shape = jax.ShapeDtypeStruct
    hidden_shape = shape((blocks, shards * block, units), bf16)
    piece = shape((width, units), bf16)
    dma = pltpu.SemaphoreType.DMA
    outs = pl.pallas_call(
        functools.partial(expert_kernel, shards),
        in_specs=[anywhere] * 5,
        out_specs=[anywhere] * 10,
        out_shape=[
            shape((members, capacity, width), bf16),
            shape((members, capacity, width), bf16),
            shape(gates.shape, f32),
            hidden_shape,
            hidden_shape,
            piece,
            piece,
            piece,
            piece,
            shape((width // 2, units), bf16),
        ],
        scratch_shapes=[
            pltpu.VMEM((blocks, block, width), bf16),
            pltpu.VMEM((blocks, block, width), bf16),
            pltpu.VMEM((block, width), bf16),
            pltpu.VMEM((2, shards * block, units), bf16),
            pltpu.VMEM((2, shards * block, units), bf16),
            pltpu.VMEM(gates.shape, f32),
            pltpu.VMEM(gates.shape, f32),
            pltpu.VMEM((block, width), f32),
            pltpu.VMEM((block, width), f32),
            pltpu.VMEM((width, hidden_units), bf16),
            pltpu.VMEM((hidden_units, width), bf16),
            pltpu.VMEM((2, width, blocks * block), bf16),
            pltpu.VMEM((2, 2, width, units), bf16),
            dma((members,)),
            dma((members,)),
            dma((members,)),
            dma((members,)),
            dma((members,)),
            dma((members,)),
            dma((members,)),
            dma((members,)),
            dma((members,)),
            dma((2,)),
            dma((2,)),
            dma((2,)),
            dma((4, blocks)),
            dma((3,)),
            dma((2, 2)),
            dma((2, 2)),
            dma((2, 4)),
            dma((2, 2)),
        ],
        compiler_params=pltpu.CompilerParams(
            collective_id=0, has_side_effects=True, vmem_limit_bytes=63 * 2**20
        ),
        cost_estimate=pl.CostEstimate(
            flops=12 * members * capacity * width * hidden_units,
            bytes_accessed=2 * (members * capacity * (6 * width + 4 * hidden_units)),
            transcendentals=members * capacity * hidden_units,
        ),
    )(sent, gates, grads, inner, outer)
    return outs[:3] + outs[5:]


def front_kernel(
    shards,
    head_dim,
    residual_ref,
    gains_ref,
    projection_piece,
    attended_piece,
    inner_piece,
    outer_piece,
    route_rows,
    out_grad_ref,
    row_ref,
    base_ref,
    router_ref,
    projection_out,
    attended_out,
    projected_out,
    merged_out,
    logs_out,
    hidden_out,
    normed_out,
    normed2_out,
    counts_out,
    sent_out,
    gates_out,
    grads_out,
    inner_out,
    outer_out,
    projection_full,
    attended_full,
    projected,
    merged,
    logs,
    hidden,
    normed,
    normed2,
    counts,
    sent,
    gate_rows,
    sent_grads,
    low_grads,
    mask_ref,
    gate_table,
    given,
    out_sems,
    local_sems,
    shared_send,
    shared_arrive,
    grad_send,
    grad_arrive,
    distant_send,
    distant_arrive,
    across_send,
    across_arrive,
    near_send,
    near_arrive,
):
    tokens, width = residual_ref.shape
    members, capacity, _ = grads_out.shape
    expert, shard = lax.axis_index("expert"), lax.axis_index("shard")
    side, half = shards // 2, members // 2
    me, device_of = group_place(members, shards)
    low, turn = lax.rem(shard, side), shard // side
    native_here = expert // half == turn
    across = {"shard": lax.rem(shard + side, shards)}
    near = {"shard": turn * side + lax.rem(low + 1, side)}
    distant = {"expert": lax.rem(expert + half, members)}
    pieces = (inner_piece, outer_piece)
    units = outer_piece.shape[0]
    per_piece = 4
    chunk_rows = width // per_piece
    chunks = range(2 * per_piece)

    def piece(index):
        start = index % per_piece * chunk_rows
        return pieces[index // per_piece].at[start : start + chunk_rows, :]

    def slot(index, which):
        place = 2 * low + which
        start = index % per_piece * chunk_rows
        if index // per_piece == 0:
            columns = pl.ds(pl.multiple_of(place * units, units), units)
            return inner_out.at[start : start + chunk_rows, columns]
        return outer_out.at[pl.ds(pl.multiple_of(place * units + start, chunk_rows), chunk_rows), :]

    def passing(index):
        start = index % per_piece * chunk_rows
        return given.at[index // per_piece, start : start + chunk_rows, :]

    def distant_copy(index, target):
        return add_remote(
            piece(index), target, distant_send.at[index], distant_arrive.at[index], distant
        )

    def across_copy(index, source):
        return add_remote(
            source, slot(index, 1), across_send.at[index], across_arrive.at[index], across
        )

    def near_copy(index, which, source):
        return add_remote(
            source,
            slot(index, which),
            near_send.at[index, which],
            near_arrive.at[index, which],
            near,
        )

    def local_copy(index):
        return pltpu.make_async_copy(piece(index), slot(index, 0), local_sems.at[index])

    def shared_rows(full, owner):
        rows = full.shape[0] // shards
        return full.at[pl.ds(pl.multiple_of(owner * rows, rows), rows), :]

    shared = ((projection_piece, projection_full), (attended_piece, attended_full))
    other = lax.rem(shard + side, shards)

    def shared_copy(index, kind):
        held, full = shared[index]
        source = shared_rows(full, other) if kind == 2 else held
        target = shared_rows(full, other if kind == 2 else shard)
        return add_remote(
            source,
            target,
            shared_send.at[index, kind],
            shared_arrive.at[index, kind],
            across if kind == 0 else near,
        )

    def shared_local(index):
        held, full = shared[index]
        return pltpu.make_async_copy(held, shared_rows(full, shard), local_sems.at[len(chunks) + index])

    def grad_copy(step):
        return add_remote(
            sent_grads.at[step],
            grads_out.at[me],
            grad_send.at[step],
            grad_arrive.at[step],
            device_of(paired(me, step, members)),
        )

    own_grads = pltpu.make_async_copy(sent_grads.at[0], grads_out.at[me], grad_send.at[0])

    def start_distant(index):
        @pl.when(native_here)
        def _():
            distant_copy(index, slot(index, 0)).start()

        @pl.when(jnp.logical_not(native_here))
        def _():
            distant_copy(index, passing(index)).start()

    def pass_on(index):
        @pl.when(native_here)
        def _():
            distant_copy(index, passing(index)).wait_recv()
            across_copy(index, passing(index)).start()
            near_copy(index, 0, piece(index)).start()

        @pl.when(jnp.logical_not(native_here))
        def _():
            distant_copy(index, slot(index, 0)).wait_recv()
            near_copy(index, 0, slot(index, 0)).start()

    def finish(index):
        across_copy(index, passing(index)).wait_recv()
        near_copy(index, 1, slot(index, 1)).start()

    def held_rows(member):
        places = lax.broadcasted_iota(jnp.int32, (capacity, tokens), 0).astype(f32)
        return (counts[pl.ds(member, 1), :] == places).astype(bf16)

    barrier = pltpu.get_barrier_semaphore()
    for device in (across, near, distant):
        pl.semaphore_signal(barrier, inc=1, device_id=device, device_id_type=mesh_ids)

    @pl.loop(1, members)
    def _(step):
        device = device_of(paired(me, step, members))
        pl.semaphore_signal(barrier, inc=1, device_id=device, device_id_type=mesh_ids)

    for index in range(2):
        shared_local(index).start()

    @pl.when(native_here)
    def _():
        for index in chunks:
            local_copy(index).start()

    pl.semaphore_wait(barrier, members + 2)
    shared_copy(0, 0).start()
    shared_copy(0, 1).start()
    for index in range(3):
        start_distant(index)
    shared_copy(1, 0).start()
    shared_copy(1, 1).start()

    tile_rows = tile

    @pl.loop(0, tokens // tile_rows)
    def _(part):
        rows = pl.ds(pl.multiple_of(part * tile_rows, tile_rows), tile_rows)
        values = residual_ref[rows, :]
        scale = lax.rsqrt(jnp.mean(values * values, axis=1, keepdims=True) + epsilon)
        normed[rows, :] = (values * scale * gains_ref[:1, :]).astype(bf16)
        low_grads[rows, :] = out_grad_ref[rows, :].astype(bf16)

    names = lax.broadcasted_iota(jnp.int32, (members, tokens), 0)
    member = (route_rows[:1, :] == names) | (route_rows[1:, :] == names)
    earlier = lax.broadcasted_iota(jnp.int32, (tokens, tokens), 0) < lax.broadcasted_iota(
        jnp.int32, (tokens, tokens), 1
    )
    ranks = dot_nn(member.astype(bf16), earlier.astype(bf16))
    counts[...] = jnp.where(member, ranks, -1.0)

    @pl.loop(0, members)
    def _(step):
        block = dot_nn(held_rows(paired(me, step, members)), low_grads[...])
        sent_grads[step] = block.astype(bf16)

    shared_copy(0, 0).wait_recv()
    shared_copy(0, 2).start()
    own_grads.start()

    @pl.loop(1, members)
    def _(step):
        grad_copy(step).start()

    column = turned_row(row_ref[...])
    for start_row in range(0, tokens, tile):
        start = key_start(start_row)
        span_width = start_row + tile - start
        others = row_ref[:, start : start_row + tile].astype(f32)
        same = column[start_row : start_row + tile, :1] == others
        ahead = lax.broadcasted_iota(jnp.int32, (tile, span_width), 1) - (start_row - start)
        later = ahead > lax.broadcasted_iota(jnp.int32, (tile, span_width), 0)
        mask_ref[start_row : start_row + tile, :span_width] = jnp.where(
            same & jnp.logical_not(later), 0.0, masked
        )
    logs[...] = jnp.zeros_like(logs)
    shared_local(0).wait()
    shared_copy(0, 1).wait_recv()
    shared_copy(0, 2).wait_recv()

    @pl.loop(0, 3 * width // tile)
    def _(part):
        columns = pl.ds(pl.multiple_of(part * tile, tile), tile)
        projected[:, columns] = dot_nn(normed[...], projection_full[:, columns]).astype(bf16)

    @pl.when(jnp.logical_not(native_here))
    def _():
        for index in chunks:
            across_copy(index, piece(index)).start()

    shared_copy(1, 0).wait_recv()
    shared_copy(1, 2).start()
    outs = (
        (projection_full, projection_out),
        (attended_full, attended_out),
        (projected, projected_out),
        (merged, merged_out),
        (logs, logs_out),
        (hidden, hidden_out),
        (normed, normed_out),
        (normed2, normed2_out),
        (counts, counts_out),
        (sent, sent_out),
        (gate_rows, gates_out),
    )

    def keep(index):
        return pltpu.make_async_copy(*outs[index], out_sems.at[index])

    for index in (0, 2, 6, 8):
        keep(index).start()
    pairs = width // lanes

    def attend(first_pair, last_pair):
        @pl.loop(first_pair, last_pair)
        def _(pair):
            columns = [
                pl.ds(pl.multiple_of(group * width + pair * lanes, lanes), lanes)
                for group in range(3)
            ]
            attend_forward_pair(
                head_dim,
                pair,
                projected.at[:, columns[0]],
                projected.at[:, columns[1]],
                projected.at[:, columns[2]],
                base_ref.at[pair],
                merged.at[:, columns[0]],
                logs,
                mask_ref,
            )

    attend(0, pairs // 2)
    for index in range(2):
        pass_on(index)
        start_distant(index + 3)
    attend(pairs // 2, pairs)
    shared_local(1).wait()
    shared_copy(1, 1).wait_recv()
    shared_copy(1, 2).wait_recv()
    for index in (1, 3, 4):
        keep(index).start()

    @pl.loop(0, width // tile)
    def _(part):
        columns = pl.ds(pl.multiple_of(part * tile, tile), tile)
        hidden[:, columns] = residual_ref[:, columns] + dot_nn(
            merged[...], attended_full[:, columns]
        )

    for index in range(2, 4):
        pass_on(index)
        start_distant(index + 3)
    keep(5).start()

    @pl.loop(0, tokens // tile_rows)
    def _(part):
        rows = pl.ds(pl.multiple_of(part * tile_rows, tile_rows), tile_rows)
        values = hidden[rows, :]
        scale = lax.rsqrt(jnp.mean(values * values, axis=1, keepdims=True) + epsilon)
        normed2[rows, :] = (values * scale * gains_ref[1:, :]).astype(bf16)

    keep(7).start()

    logits = dot_nt(router_ref[...], normed2[...])[:members, :]
    first, second = route_rows[:1, :] == names, route_rows[1:, :] == names
    lean = jnp.sum(jnp.where(first, logits, 0.0), axis=0, keepdims=True)
    lean = lean - jnp.sum(jnp.where(second, logits, 0.0), axis=0, keepdims=True)
    gate_table[...] = jnp.where(first, jax.nn.sigmoid(lean), 0.0) + jnp.where(
        second, jax.nn.sigmoid(-lean), 0.0
    )
    gate_rows[...] = jnp.zeros_like(gate_rows)

    @pl.loop(0, members)
    def _(member_index):
        held = held_rows(member_index)
        sent[member_index] = dot_nn(held, normed2[...]).astype(bf16)
        digits = split_digits(gate_table[pl.ds(member_index, 1), :])
        sums = jnp.sum(dot_nt(digits, held), axis=0, keepdims=True)
        gate_rows[member_index, :1, :capacity] = sums

    keep(9).start()
    keep(10).start()
    for index in range(4):
        finish(index)
    for index in range(4, 8):
        pass_on(index)
        if index + 3 < len(chunks):
            start_distant(index + 3)
        if index > 4:
            finish(index - 1)
    finish(len(chunks) - 1)

    own_grads.wait()

    @pl.loop(1, members)
    def _(step):
        grad_copy(step).wait()

    for index in range(len(outs)):
        keep(index).wait()
    for index in range(2):
        for kind in range(3):
            shared_copy(index, kind).wait_send()
    for index in chunks:
        distant_copy(index, passing(index)).wait_send()
        across_copy(index, passing(index)).wait_send()
        for which in range(2):
            near_copy(index, which, slot(index, which)).wait()

    @pl.when(native_here)
    def _():
        for index in chunks:
            local_copy(index).wait()


def run_front(
    residual_in,
    gains,
    projection_piece,
    attended_piece,
    inner_piece,
    outer_piece,
    route_rows,
    out_grad,
    marks,
    base_rows,
    router_turned,
    capacity,
    members,
    shards,
):
    tokens, width = residual_in.shape
    wide = projection_piece.shape[1]
    heads = base_rows.shape[0]
    pairs = width // lanes
    units = outer_piece.shape[0]
    whole = pl.BlockSpec(memory_space=pltpu.VMEM)
    anywhere = pl.BlockSpec(memory_space=pl.ANY)
    shape = jax.ShapeDtypeStruct
    held = [
        ((shards * projection_piece.shape[0], wide), bf16),
        ((shards * attended_piece.shape[0], width), bf16),
        ((tokens, wide), bf16),
        ((tokens, width), bf16),
        ((tokens, lanes), f32),
        ((tokens, width), f32),
        ((tokens, width), bf16),
        ((tokens, width), bf16),
        ((members, tokens), f32),
        ((members, capacity, width), bf16),
        ((members, 8, -(-capacity // lanes) * lanes), f32),
    ]
    dma = pltpu.SemaphoreType.DMA
    return pl.pallas_call(
        functools.partial(front_kernel, shards, width // heads),
        in_specs=[whole] * 2 + [anywhere] * 4 + [whole] * 5,
        out_specs=[anywhere] * 14,
        out_shape=[shape(*entry) for entry in held]
        + [
            shape((members, capacity, width), bf16),
            shape((width, shards * units), bf16),
            shape((shards * units, width), bf16),
        ],
        scratch_shapes=[pltpu.VMEM(*entry) for entry in held]
        + [
            pltpu.VMEM((members, capacity, width), bf16),
            pltpu.VMEM((tokens, width), bf16),
            pltpu.VMEM((tokens, span), f32),
            pltpu.VMEM((members, tokens), f32),
            pltpu.VMEM((2, units, width), bf16),
            dma((len(held),)),
            dma((10,)),
            dma((2, 3)),
            dma((2, 3)),
            dma((members,)),
            dma((members,)),
            dma((8,)),
            dma((8,)),
            dma((8,)),
            dma((8,)),
            dma((8, 2)),
            dma((8, 2)),
        ],
        compiler_params=pltpu.CompilerParams(
            collective_id=2, has_side_effects=True, vmem_limit_bytes=60 * 2**20
        ),
        cost_estimate=pl.CostEstimate(
            flops=2 * tokens * width * (wide + width) + 4 * members * capacity * tokens * width,
            bytes_accessed=20 * tokens * width,
            transcendentals=heads * tokens * tokens // 2,
        ),
    )(
        residual_in,
        gains,
        projection_piece,
        attended_piece,
        inner_piece,
        outer_piece,
        route_rows,
        out_grad,
        marks[None, :],
        base_rows.reshape(pairs, heads // pairs, span),
        router_turned,
    )


def held_tile(counts, capacity):
    places = lax.broadcasted_iota(jnp.int32, (capacity, counts.shape[1]), 0).astype(f32)
    blocks = [
        (counts[member : member + 1, :] == places).astype(bf16)
        for member in range(counts.shape[0])
    ]
    return jnp.concatenate(blocks, axis=0)


def row_scale(values):
    return lax.rsqrt(jnp.mean(values * values, axis=1, keepdims=True) + epsilon)


def back_kernel(
    shards,
    members,
    head_dim,
    capacity,
    reduce_here,
    projected,
    logs,
    row_ref,
    route_rows,
    base_ref,
    normed,
    normed2,
    merged,
    projection_full,
    attended_full,
    router_ref,
    gains_ref,
    counts_ref,
    gates_back,
    back_ref,
    out_grad_ref,
    gated_ref,
    residual_ref,
    hidden_ref,
    inner_mine,
    inner_crossed,
    outer_mine,
    outer_given,
    inner_distant,
    residual_out,
    block_out,
    projection_out,
    attended_out,
    small_out,
    inner_final,
    outer_final,
    distant_in,
    outer_crossed,
    hidden_grad_ref,
    mask_ref,
    log_turned,
    dk_total,
    dv_total,
    diagonal,
    grads,
    merged_grad,
    attended_grad,
    attended_part,
    bias_rows,
    parts,
    first_in,
    second_in,
    results_tile,
    results_ref,
    near_in,
    far_in,
    halves,
    half_in,
    quads,
    quad_in,
    pieces,
    piece_in,
    finished,
    finished_in,
    quad_back,
    half_back,
    small_own,
    small_in,
    small_sum,
    stream_sems,
    distant_sems,
    across_sems,
    near_sems,
    far_sems,
    half_sems,
    back_sems,
    quad_sems,
    piece_sems,
    finished_sems,
    quad_back_sems,
    small_sems,
    result_send,
    result_arrive,
    back_load_sems,
    final_sems,
):
    tokens, width = normed.shape
    pairs = width // lanes
    group = width // shards
    expert, shard = lax.axis_index("expert"), lax.axis_index("shard")
    side, half = shards // 2, members // 2
    low, turn = lax.rem(shard, side), shard // side
    native_here = expert // half == turn
    across = {"shard": lax.rem(shard + side, shards)}
    near = {"shard": turn * side + lax.rem(low + 1, side)}
    distant = {"expert": lax.rem(expert + half, members)}
    odd, level = lax.rem(expert, 2), expert // 2
    beside = {"expert": expert + 1 - 2 * odd}
    low_level, top_level = lax.rem(level, 2), level // 2
    above = {"expert": (level + 1 - 2 * low_level) * 2 + odd}
    high, wide = group // 4, width // 2
    own_columns = pl.ds(pl.multiple_of(top_level * wide, lanes), wide)
    other_columns = pl.ds(pl.multiple_of((1 - top_level) * wide, lanes), wide)

    def distant_copy(matrix, source):
        top = width // 2 if matrix == 0 else 0
        return add_remote(
            source.at[top:, :],
            distant_in.at[matrix, top:, :],
            distant_sems.at[0, matrix],
            distant_sems.at[1, matrix],
            distant,
        )

    across_copy = add_remote(
        outer_given, outer_crossed, across_sems.at[0], across_sems.at[1], across
    )
    part_refs = [attended_part] + [parts.at[index] for index in range(3)]
    me, device_of = group_place(members, shards)

    def result_rows():
        start = pl.multiple_of(me * capacity, 16)
        return results_ref.at[pl.ds(start, capacity), :]

    def result_copy(step):
        member = paired(me, step, members)
        return add_remote(
            gated_ref.at[member],
            result_rows(),
            result_send.at[step],
            result_arrive.at[step],
            device_of(member),
        )

    own_result = pltpu.make_async_copy(gated_ref.at[me], result_rows(), result_send.at[0])
    count = len(part_refs)

    def near_copy(index, top):
        start = pl.multiple_of((2 * top + 1 - low) * group, group)
        return add_remote(
            part_refs[index].at[pl.ds(start, group), :],
            near_in.at[index, top],
            near_sems.at[0, index, top],
            near_sems.at[1, index, top],
            near,
        )

    def far_copy(index):
        return add_remote(
            near_in.at[index, 1 - turn],
            far_in.at[index],
            far_sems.at[0, index],
            far_sems.at[1, index],
            across,
        )

    def half_copy(index):
        return add_remote(
            halves.at[index, 1 - odd],
            half_in.at[index],
            half_sems.at[0, index],
            half_sems.at[1, index],
            beside,
        )

    def quad_copy(index):
        return add_remote(
            quads.at[index, 1 - low_level],
            quad_in.at[index],
            quad_sems.at[0, index],
            quad_sems.at[1, index],
            above,
        )

    def piece_copy(index):
        return add_remote(
            pieces.at[index, 1 - top_level],
            piece_in.at[index],
            piece_sems.at[0, index],
            piece_sems.at[1, index],
            distant,
        )

    def finished_copy(index):
        return add_remote(
            finished.at[index],
            finished_in.at[index],
            finished_sems.at[0, index],
            finished_sems.at[1, index],
            distant,
        )

    def quad_back_copy(index):
        return add_remote(
            quads.at[index, low_level],
            quad_back.at[index],
            quad_back_sems.at[0, index],
            quad_back_sems.at[1, index],
            above,
        )

    def back_copy(index):
        return add_remote(
            halves.at[index, odd],
            half_back.at[index],
            back_sems.at[0, index],
            back_sems.at[1, index],
            beside,
        )

    def small_copy(stage):
        return add_remote(
            small_own if stage == 0 else small_sum.at[stage - 1],
            small_in.at[stage],
            small_sems.at[0, stage],
            small_sems.at[1, stage],
            (near, across, beside, above, distant)[stage],
        )

    def start_near(index):
        if reduce_here:
            for top in range(2):
                near_copy(index, top).start()

    def near_to_far(index):
        if reduce_here:
            for top in range(2):
                near_copy(index, top).wait_recv()
                start = pl.multiple_of((2 * top + low) * group, group)
                own = part_refs[index][pl.ds(start, group), :].astype(f32)
                near_in[index, top] = (own + near_in[index, top].astype(f32)).astype(bf16)
            far_copy(index).start()

    def far_to_half(index):
        if reduce_here:
            far_copy(index).wait_recv()
            total = near_in[index, turn].astype(f32) + far_in[index].astype(f32)
            total = total.astype(bf16)
            for place in range(2):
                halves[index, place] = total[2 * place * high : 2 * (place + 1) * high, :]
            half_copy(index).start()

    def half_to_quad(index):
        if reduce_here:
            half_copy(index).wait_recv()
            total = halves[index, odd].astype(f32) + half_in[index].astype(f32)
            total = total.astype(bf16)
            for place in range(2):
                quads[index, place] = total[place * high : (place + 1) * high, :]
            quad_copy(index).start()

    def quad_to_piece(index):
        if reduce_here:
            quad_copy(index).wait_recv()
            total = quads[index, low_level].astype(f32) + quad_in[index].astype(f32)
            total = total.astype(bf16)
            for place in range(2):
                pieces[index, place] = total[:, place * wide : (place + 1) * wide]
            piece_copy(index).start()

    def piece_to_finished(index):
        if reduce_here:
            piece_copy(index).wait_recv()
            total = pieces[index, top_level].astype(f32) + piece_in[index].astype(f32)
            finished[index] = total.astype(bf16)
            finished_copy(index).start()

    def finished_to_quad(index):
        if reduce_here:
            finished_copy(index).wait_recv()
            quads[index, low_level, :, own_columns] = finished[index]
            quads[index, low_level, :, other_columns] = finished_in[index]
            quad_back_copy(index).start()

    def quad_to_back(index):
        if reduce_here:
            quad_back_copy(index).wait_recv()
            own = pl.ds(pl.multiple_of(low_level * high, 16), high)
            other = pl.ds(pl.multiple_of((1 - low_level) * high, 16), high)
            halves[index, odd, own, :] = quads[index, low_level]
            halves[index, odd, other, :] = quad_back[index]
            back_copy(index).start()

    def write_out(index):
        if reduce_here:
            back_copy(index).wait_recv()
            for place, block in ((odd, halves.at[index, odd]), (1 - odd, half_back.at[index])):
                rows = pl.ds(pl.multiple_of(place * 2 * high, 2 * high), 2 * high)
                values = block[...].astype(f32)
                if index == 0:
                    attended_out[rows, :] = values
                else:
                    projection_out[rows, (index - 1) * width : index * width] = values

    def small_step(stage):
        if reduce_here:
            small_copy(stage).wait_recv()
            own = small_own[...] if stage == 0 else small_sum[stage - 1]
            small_sum[stage] = own + small_in[stage]
            if stage < 4:
                small_copy(stage + 1).start()

    barrier = pltpu.get_barrier_semaphore()
    partners = [across, distant]
    if reduce_here:
        partners = [across, near, beside, above, distant]
    for device in partners:
        pl.semaphore_signal(barrier, inc=1, device_id=device, device_id_type=mesh_ids)

    @pl.loop(1, members)
    def _(step):
        device = device_of(paired(me, step, members))
        pl.semaphore_signal(barrier, inc=1, device_id=device, device_id_type=mesh_ids)

    own_result.start()
    pl.semaphore_wait(barrier, len(partners) + members - 1)

    across_copy.start()

    @pl.when(native_here)
    def _():
        distant_copy(0, inner_crossed).start()

    @pl.when(jnp.logical_not(native_here))
    def _():
        distant_copy(0, inner_mine).start()
        distant_copy(1, outer_mine).start()

    def load_rows(source, target, part, kind):
        return pltpu.make_async_copy(
            source.at[part * tile : (part + 1) * tile, :],
            target.at[part % 2],
            stream_sems.at[kind, part % 2],
        )

    def store_rows(target, part):
        return pltpu.make_async_copy(
            results_tile.at[part % 2],
            target.at[part * tile : (part + 1) * tile, :],
            stream_sems.at[2, part % 2],
        )

    row_parts = tokens // tile
    back_count = members * capacity
    back_loads = [
        pltpu.make_async_copy(
            back_ref.at[top : min(top + tokens, back_count), :],
            grads.at[top // tokens, : min(tokens, back_count - top), :],
            back_load_sems.at[top // tokens],
        )
        for top in range(0, back_count, tokens)
    ]
    for copy in back_loads:
        copy.start()
    for part in range(2):
        load_rows(hidden_ref, first_in, part, 0).start()
        load_rows(out_grad_ref, second_in, part, 1).start()

    log_turned[...] = logs[...].T
    column = turned_row(row_ref[...])
    for first in range(0, tokens, tile):
        start = key_start(first)
        span_width = first + tile - start
        own_marks = row_ref[:, first : first + tile].astype(f32)
        same = column[start : first + tile, :1] == own_marks
        ahead = lax.broadcasted_iota(jnp.int32, (span_width, tile), 0) - (first - start)
        later = ahead > lax.broadcasted_iota(jnp.int32, (span_width, tile), 1)
        mask_ref[:span_width, first : first + tile] = jnp.where(
            same & jnp.logical_not(later), 0.0, masked
        )
    small_own[...] = jnp.zeros_like(small_own)
    bias_top = small_own.shape[0] - pairs * bias_rows.shape[1]
    lane = lax.broadcasted_iota(jnp.int32, (tile, lanes), 1).astype(f32)
    for copy in back_loads:
        copy.wait()

    def middle_rows(part):
        rows = slice(part * tile, (part + 1) * tile)
        held = held_tile(counts_ref[:, rows], capacity)
        combined = functools.reduce(
            jnp.add,
            [
                dot_tn(
                    held[top : min(top + tokens, back_count), :],
                    grads[top // tokens, : min(tokens, back_count - top), :],
                )
                for top in range(0, back_count, tokens)
            ],
        )
        first, second = route_rows[:1, rows], route_rows[1:, rows]
        difference = jnp.zeros((1, tile), f32)
        for member in range(members):
            digits = split_digits(gates_back[member, :1, :capacity])
            sums = dot_nn(digits, held[member * capacity : (member + 1) * capacity, :])
            sums = jnp.sum(sums, axis=0, keepdims=True)
            difference = difference + jnp.where(jnp.minimum(first, second) == member, sums, -sums)
        difference = turned_row(difference)[:, :1]
        first, second = turned_row(first)[:, :1], turned_row(second)[:, :1]
        least, most = jnp.minimum(first, second), jnp.maximum(first, second)
        signs = (lane == least).astype(f32) - (lane == most).astype(f32)
        values = normed2[rows, :]
        lean = jnp.sum(dot_nt(values, router_ref[...]) * signs, axis=1, keepdims=True)
        gates = jax.nn.sigmoid(lean)
        logit_grad = gates * (1.0 - gates) * difference * signs
        above = logit_grad.astype(bf16)
        below = (logit_grad - above.astype(f32)).astype(bf16)
        router_grad = dot_tn(above, values) + dot_tn(below, values)
        small_own[2:bias_top, :] += router_grad[: bias_top - 2, :]
        gradient = dot_nn(above, router_ref[...]) + dot_nn(below, router_ref[...]) + combined
        load_rows(hidden_ref, first_in, part, 0).wait()
        load_rows(out_grad_ref, second_in, part, 1).wait()
        hidden = first_in[part % 2]
        scale = row_scale(hidden)
        weighted = gradient * gains_ref[1:, :]
        inner = jnp.mean(weighted * hidden, axis=1, keepdims=True)
        small_own[1:2, :] += jnp.sum(gradient * hidden * scale, axis=0, keepdims=True)
        if part >= 2:
            store_rows(hidden_grad_ref, part - 2).wait()
        hidden_grad = (
            second_in[part % 2] + scale * weighted - hidden * (scale * scale * scale * inner)
        )
        results_tile[part % 2] = hidden_grad
        store_rows(hidden_grad_ref, part).start()
        if part + 2 < row_parts:
            load_rows(hidden_ref, first_in, part + 2, 0).start()
            load_rows(out_grad_ref, second_in, part + 2, 1).start()
        low_grad = hidden_grad.astype(bf16)
        attended_grad[rows, :] = low_grad
        merged_grad[rows, :] = dot_nt(low_grad, attended_full[...]).astype(bf16)

    for part in range(row_parts):
        middle_rows(part)

    @pl.loop(0, width // tile)
    def _(part):
        columns = pl.ds(pl.multiple_of(part * tile, tile), tile)
        attended_part[:, columns] = dot_tn(merged[...], attended_grad[:, columns]).astype(bf16)

    start_near(0)
    for part in range(row_parts - 2, row_parts):
        store_rows(hidden_grad_ref, part).wait()

    def attend(first_pair, last_pair):
        @pl.loop(first_pair, last_pair)
        def _(pair):
            columns = [
                pl.ds(pl.multiple_of(place * width + pair * lanes, lanes), lanes)
                for place in range(3)
            ]
            own = columns[0]
            attend_backward_pair(
                head_dim,
                pair,
                projected.at[:, columns[0]],
                projected.at[:, columns[1]],
                projected.at[:, columns[2]],
                merged_grad.at[:, own],
                base_ref.at[pair],
                grads.at[0, :, own],
                grads.at[1, :, own],
                grads.at[2, :, own],
                bias_rows.at[pair],
                mask_ref,
                log_turned,
                dk_total,
                dv_total,
                diagonal,
            )

    @pl.loop(1, members)
    def _(step):
        result_copy(step).start()

    attend(0, pairs // 2)
    near_to_far(0)

    @pl.when(native_here)
    def _():
        across_copy.wait_recv()
        distant_copy(1, outer_crossed).start()

    attend(pairs // 2, pairs)
    far_to_half(0)
    for index in range(3):
        @pl.loop(0, width // tile)
        def _(part):
            columns = pl.ds(pl.multiple_of(part * tile, tile), tile)
            parts[index, :, columns] = dot_tn(normed[...], grads[index, :, columns]).astype(bf16)

        start_near(index + 1)
    per_pair = bias_rows.shape[1]
    for pair in range(pairs):
        top = bias_top + pair * per_pair
        small_own[top : top + per_pair, :] = bias_rows[pair]

    def norm_rows(part):
        rows = slice(part * tile, (part + 1) * tile)
        normed_grad = functools.reduce(
            jnp.add,
            [
                dot_nt(grads[index, rows, :], projection_full[:, index * width : (index + 1) * width])
                for index in range(3)
            ],
        )
        load_rows(residual_ref, first_in, part, 0).wait()
        load_rows(hidden_grad_ref, second_in, part, 1).wait()
        values = first_in[part % 2]
        scale = row_scale(values)
        weighted = normed_grad * gains_ref[:1, :]
        inner = jnp.mean(weighted * values, axis=1, keepdims=True)
        if part >= 2:
            store_rows(residual_out, part - 2).wait()
        results_tile[part % 2] = (
            second_in[part % 2] + scale * weighted - values * (scale * scale * scale * inner)
        )
        small_own[:1, :] += jnp.sum(normed_grad * values * scale, axis=0, keepdims=True)
        store_rows(residual_out, part).start()
        if part + 2 < tokens // tile:
            load_rows(residual_ref, first_in, part + 2, 0).start()
            load_rows(hidden_grad_ref, second_in, part + 2, 1).start()
        else:
            load_rows(hidden_ref, first_in, part % 2, 0).start()

    def block_rows(part):
        held = held_tile(counts_ref[:, part * tile : (part + 1) * tile], capacity)
        sums = dot_tn(held, results_ref[...])
        load_rows(hidden_ref, first_in, part, 0).wait()
        if part < 2:
            store_rows(residual_out, tokens // tile - 2 + part).wait()
        else:
            store_rows(block_out, part - 2).wait()
        results_tile[part % 2] = first_in[part % 2] + sums
        store_rows(block_out, part).start()
        if part + 2 < tokens // tile:
            load_rows(hidden_ref, first_in, part + 2, 0).start()

    def final_load(matrix, source, kind):
        target = (attended_grad, merged_grad)[kind]
        return pltpu.make_async_copy(source, target.at[:width, :], final_sems.at[matrix, kind])

    def start_final(matrix):
        mine, crossed = ((inner_mine, inner_crossed), (outer_mine, outer_crossed))[matrix]

        @pl.when(native_here)
        def _():
            final_load(matrix, mine, 0).start()

        @pl.when(jnp.logical_not(native_here))
        def _():
            if matrix == 1:
                across_copy.wait_recv()
            final_load(matrix, crossed, 0).start()

        distant_copy(matrix, inner_mine).wait_recv()
        for copy in distant_loads(matrix):
            copy.start()

    def distant_loads(matrix):
        middle = width // 2
        if matrix == 1:
            return [final_load(1, distant_in.at[1], 1)]
        return [
            pltpu.make_async_copy(
                inner_distant, merged_grad.at[:middle, :], final_sems.at[0, 1]
            ),
            pltpu.make_async_copy(
                distant_in.at[0, middle:, :],
                merged_grad.at[middle:width, :],
                final_sems.at[1, 3],
            ),
        ]

    final_stores = [
        pltpu.make_async_copy(
            diagonal.at[0], inner_final.at[: 2 * tile, :], final_sems.at[0, 2]
        ),
        pltpu.make_async_copy(
            diagonal.at[1, :tile, :], inner_final.at[2 * tile :, :], final_sems.at[0, 3]
        ),
        pltpu.make_async_copy(mask_ref.at[:, :width], outer_final, final_sems.at[1, 2]),
    ]

    def finish_final(matrix):
        for copy in [final_load(matrix, inner_mine, 0)] + distant_loads(matrix):
            copy.wait()
        for part in range(3):
            lines = slice(part * tile, (part + 1) * tile)
            sums = attended_grad[lines, :].astype(f32) + merged_grad[lines, :].astype(f32)
            if matrix == 1:
                mask_ref[:, lines] = sums.T
            else:
                diagonal[part // 2, part % 2 * tile : (part % 2 + 1) * tile, :] = sums
        for copy in final_stores[2:] if matrix == 1 else final_stores[:2]:
            copy.start()

    chunks = range(1, count)
    for part in range(2):
        load_rows(residual_ref, first_in, part, 0).start()
        load_rows(hidden_grad_ref, second_in, part, 1).start()
    half_to_quad(0)
    for index in chunks:
        near_to_far(index)
    for part in range(row_parts // 2):
        norm_rows(part)
    quad_to_piece(0)
    for index in chunks:
        far_to_half(index)
    for part in range(row_parts // 2, row_parts):
        norm_rows(part)
    if reduce_here:
        small_copy(0).start()
    piece_to_finished(0)
    for index in chunks:
        half_to_quad(index)
    own_result.wait()

    @pl.loop(1, members)
    def _(step):
        result_copy(step).wait()

    block_rows(0)
    small_step(0)
    for index in chunks:
        quad_to_piece(index)
    finished_to_quad(0)
    block_rows(1)
    small_step(1)
    for index in chunks:
        piece_to_finished(index)
    start_final(0)
    block_rows(2)
    small_step(2)
    quad_to_back(0)
    for index in chunks:
        finished_to_quad(index)
    for part in range(3, row_parts):
        block_rows(part)
    small_step(3)
    finish_final(0)
    for index in chunks:
        quad_to_back(index)
    small_step(4)
    start_final(1)
    finish_final(1)
    for index in range(count):
        write_out(index)
    if reduce_here:
        small_out[...] = small_sum[4]
    else:
        small_out[...] = small_own[...]
        for index in range(3):
            projection_out[:, index * width : (index + 1) * width] = parts[index]
        attended_out[...] = attended_part[...]

    for part in range(row_parts - 2, row_parts):
        store_rows(block_out, part).wait()
    across_copy.wait_send()
    for matrix in range(2):
        distant_copy(matrix, inner_mine).wait_send()
    for copy in final_stores:
        copy.wait()
    if reduce_here:
        for index in range(count):
            for top in range(2):
                near_copy(index, top).wait_send()
            far_copy(index).wait_send()
            back_copy(index).wait_send()
            half_copy(index).wait_send()
            quad_copy(index).wait_send()
            piece_copy(index).wait_send()
            finished_copy(index).wait_send()
            quad_back_copy(index).wait_send()
        for stage in range(5):
            small_copy(stage).wait_send()


def run_back(
    projected,
    logs,
    marks,
    route_rows,
    base_turned,
    normed,
    normed2,
    merged,
    projection_full,
    attended_full,
    router,
    gains,
    counts,
    gates_back,
    back,
    out_grad,
    gated,
    residual_in,
    hidden,
    weights,
    capacity,
    members,
    shards,
):
    tokens, width = normed.shape
    heads = base_turned.shape[0]
    pairs = width // lanes
    per_pair = heads // pairs
    group = width // shards
    units = weights[0].shape[1]
    small_shape = (-(-(2 + members + heads) // 8) * 8, width)
    reduce_here = members == 8 and shards == 4 and group % 64 == 0 and width % 256 == 0
    high, wide = group // 4, width // 2
    whole = pl.BlockSpec(memory_space=pltpu.VMEM)
    anywhere = pl.BlockSpec(memory_space=pl.ANY)
    shape = jax.ShapeDtypeStruct
    if reduce_here:
        sums = [shape((group, 3 * width), f32), shape((group, width), f32)]
    else:
        sums = [shape((width, 3 * width), bf16), shape((width, width), bf16)]
        high, wide = 16, lanes
    count = 4
    dma = pltpu.SemaphoreType.DMA
    vmem = pltpu.VMEM
    piece = (count, high, wide)
    quad = (count, high, 2 * wide)
    outs = pl.pallas_call(
        functools.partial(
            back_kernel, shards, members, width // heads, capacity, reduce_here
        ),
        in_specs=[whole] * 14 + [anywhere] * 10,
        out_specs=[anywhere] * 2 + [whole] * 3 + [anywhere] * 5,
        out_shape=[shape((tokens, width), f32)] * 2
        + sums
        + [
            shape(small_shape, f32),
            shape((width, units), f32),
            shape((units, width), f32),
            shape((2, width, units), bf16),
            shape((width, units), bf16),
            shape((tokens, width), f32),
        ],
        scratch_shapes=[
            vmem((span, tokens), f32),
            vmem((lanes, tokens), f32),
            vmem((tokens, lanes), f32),
            vmem((tokens, lanes), f32),
            vmem((per_pair, 2 * tile, span), f32),
            vmem((3, tokens, width), bf16),
            vmem((tokens, width), bf16),
            vmem((tokens, width), bf16),
            vmem((width, width), bf16),
            vmem((pairs, per_pair, span), f32),
            vmem((3, width, width), bf16),
            vmem((2, tile, width), f32),
            vmem((2, tile, width), f32),
            vmem((2, tile, width), f32),
            vmem((members * capacity, width), bf16),
            vmem((count, 2, group, width), bf16),
            vmem((count, group, width), bf16),
            vmem((count, 2, 2 * high, 2 * wide), bf16),
            vmem((count, 2 * high, 2 * wide), bf16),
            vmem((count, 2, high, 2 * wide), bf16),
            vmem(quad, bf16),
            vmem((count, 2, high, wide), bf16),
            vmem(piece, bf16),
            vmem(piece, bf16),
            vmem(piece, bf16),
            vmem(quad, bf16),
            vmem((count, 2 * high, 2 * wide), bf16),
            vmem(small_shape, f32),
            vmem((5,) + small_shape, f32),
            vmem((5,) + small_shape, f32),
            dma((3, 2)),
            dma((2, 2)),
            dma((2,)),
            dma((2, count, 2)),
            dma((2, count)),
            dma((2, count)),
            dma((2, count)),
            dma((2, count)),
            dma((2, count)),
            dma((2, count)),
            dma((2, count)),
            dma((2, 5)),
            dma((members,)),
            dma((members,)),
            dma((4,)),
            dma((2, 4)),
        ],
        compiler_params=pltpu.CompilerParams(
            collective_id=4, has_side_effects=True, vmem_limit_bytes=62 * 2**20
        ),
        cost_estimate=pl.CostEstimate(
            flops=16 * tokens * tokens * width,
            bytes_accessed=40 * tokens * width,
            transcendentals=heads * tokens * tokens // 2,
        ),
    )(
        projected,
        logs,
        marks[None, :],
        route_rows,
        base_turned.reshape(pairs, per_pair, span),
        normed,
        normed2,
        merged,
        projection_full,
        attended_full,
        router,
        gains,
        counts,
        gates_back,
        back,
        out_grad,
        gated,
        residual_in,
        hidden,
        *weights,
    )
    return outs[:-3], reduce_here


def sum_rows(part):
    return lax.all_gather(
        lax.psum_scatter(part.astype(bf16), ("shard", "expert"), scatter_dimension=0, tiled=True),
        "expert",
        axis=0,
        tiled=True,
    ).astype(f32)


def per_device(
    residual_in,
    norm1_gain,
    w_projection,
    rel_bias,
    w_attn_out,
    norm2_gain,
    w_router,
    expert_in,
    expert_out,
    segments,
    routes,
    out_grad,
):
    highest = lax.Precision.HIGHEST
    tokens_here, width = residual_in.shape
    heads, buckets = rel_bias.shape
    experts_all = w_router.shape[1]
    capacity = -(-5 * tokens_here // (32 * experts_all)) * 16
    marks = segments.reshape(-1)
    experts = jnp.arange(experts_all, dtype=jnp.int32)
    table_rows, table_turned = bias_tables(buckets)

    gains = jnp.stack([norm1_gain, norm2_gain])
    router = jnp.pad(w_router.T, ((0, -experts_all % lanes), (0, 0)))
    route_rows = routes.T
    base_rows = jnp.dot(rel_bias, table_rows.T, precision=highest)
    base_turned = jnp.dot(rel_bias, table_turned.T, precision=highest)
    (
        full_projection,
        full_attn_out,
        projected,
        merged,
        logs,
        hidden,
        normed,
        normed2,
        counts,
        sent,
        gate_rows,
        arrived_grad,
        inner,
        outer,
    ) = run_front(
        residual_in,
        gains,
        w_projection,
        w_attn_out,
        expert_in[0],
        expert_out[0],
        route_rows,
        out_grad,
        marks,
        base_rows,
        router,
        capacity,
        experts_all,
        lax.axis_size("shard"),
    )
    shards = lax.axis_size("shard")
    gated, back_rows, gates_back, *weights = run_experts(
        sent, gate_rows, arrived_grad, inner, outer, shards
    )
    inner_mine, outer_mine, outer_given, inner_crossed, inner_distant = weights
    filled = 2 + experts_all
    outs, reduced = run_back(
        projected,
        logs,
        marks,
        route_rows,
        base_turned,
        normed,
        normed2,
        merged,
        full_projection,
        full_attn_out,
        router,
        gains,
        counts,
        gates_back,
        back_rows.reshape(-1, width),
        out_grad,
        gated,
        residual_in,
        hidden,
        (inner_mine, inner_crossed, outer_mine, outer_given, inner_distant),
        capacity,
        experts_all,
        shards,
    )
    residual_grad, block_out, projection_total, attn_out_total, small = outs[:5]
    expert_in_grad, expert_out_grad = outs[5:]
    if not reduced:
        projection_total = sum_rows(projection_total)
        attn_out_total = sum_rows(attn_out_total)
        small = lax.psum(small, ("expert", "shard"))
    gain1_total, gain2_total = small[0], small[1]
    router_total = small[2:filled].T
    bias_total = jnp.dot(small[small.shape[0] - heads :], table_turned, precision=highest)
    return (
        block_out,
        residual_grad,
        gain1_total,
        projection_total,
        bias_total,
        attn_out_total,
        gain2_total,
        router_total,
        expert_in_grad[None],
        expert_out_grad[None],
    )


def solution(mesh):
    return jax.shard_map(
        per_device,
        mesh=mesh,
        in_specs=(
            P(("expert", "shard"), None),
            P(),
            P("shard", None),
            P(),
            P("shard", None),
            P(),
            P(),
            P("expert", None, "shard"),
            P("expert", "shard", None),
            P(("expert", "shard"), None),
            P(("expert", "shard"), None),
            P(("expert", "shard"), None),
        ),
        out_specs=(
            P(("expert", "shard"), None),
            P(("expert", "shard"), None),
            P(),
            P("shard", None),
            P(),
            P("shard", None),
            P(),
            P(),
            P("expert", None, "shard"),
            P("expert", "shard", None),
        ),
        check_vma=False,
    )
```

time: 3110 us -> 466 us (0.15)
  local copies, waits for them, and re-layouts: 1720 us -> 18.9 us
  Pallas kernels: 0 us -> 434 us
  matrix products: 394 us -> 2.97 us
  waiting for transfers between devices: 380 us -> 0 us
  blocking collectives: 326 us -> 0 us
  other arithmetic: 223 us -> 0.6 us
    reshape x6 -> x2, local copies, waits for them, and re-layouts: 586 us -> 1.28 us  [the longest x1 0.64 us: run_front(): base_rows.reshape(pairs, heads // pairs, span)]
    while x70 -> x0, local copies, waits for them, and re-layouts: 499 us -> none
    pallas_call x0 -> x3, Pallas kernels: none -> 434 us  [the longest x1 152 us: run_experts(): pl.pallas_call(functools.partial(expert_kernel, shards), in_specs=[anywhe...]
    dot_general x32 -> x3, matrix products: 394 us -> 2.97 us  [the longest x1 1.72 us: per_device(): jnp.dot(small[small.shape[0] - heads:], table_turned, precision=highest)]
    dynamic_update_slice x2 -> x0, local copies, waits for them, and re-layouts: 249 us -> none  [diagonal_sums(): lax.dynamic_update_slice_in_dim(placed, score_grad, seq_len - 1 - offset, 2)]
    reduce_scatter x4 -> x0, waiting for transfers between devices: 215 us -> none  [the longest x1 117 us: per_device(): lax.psum_scatter(partial_value.astype(jnp.bfloat16), 'shard', scatter_dim...]
    all_to_all x2 -> x0, blocking collectives: 185 us -> none  [the longest x1 93.7 us: per_device(): lax.all_to_all(outgoing, 'expert', split_axis=0, concat_axis=0, tiled=True)]
    slice x8 -> x1, local copies, waits for them, and re-layouts: 186 us -> 1.43 us  [per_device(): gain1_total, gain2_total = (small[0], small[1])]
  transfers between devices with their start and end apart: 10 -> 0, of which waited for: 5 -> 0; matrix products, arithmetic and copies ran while one was open for 71% -> 0% of each run, Pallas kernels for 0% -> 0%
where the time goes in v1:
time: 466 us; the launch traced here: 458 us
  Pallas kernels  434 us (93%)
  local copies, waits for them, and re-layouts  18.9 us (4%)
    pallas_call x1, Pallas kernels, run_experts(): pl.pallas_call(functools.partial(expert_kernel, shards), in_specs=[anywhe...  152 us
    pallas_call x1, Pallas kernels, run_back(): pl.pallas_call(functools.partial(back_kernel, shards, members, width // h...  152 us
    pallas_call x1, Pallas kernels, run_front(): pl.pallas_call(functools.partial(front_kernel, shards, width // heads), i...  130 us
    unnamed x22, local copies, waits for them, and re-layouts  12 us

profile of v1, /device:TPU:0, one launch (start us, length us, event | category | flops | bytes accessed | tf_op | source)
XLA Modules:
  0.0 457.7 jit_solution(8864833863148365319)
XLA Ops:
  0.6 0.0 copy-start
  0.7 1.4 pad.4.router_ref
  2.1 0.7 stack.10
  2.7 0.7 stack.9
  3.4 0.6 pad_maximum_fusion.gains_ref
  4.0 1.1 convolution_bitcast_fusion.1
  5.1 0.6 reshape.29.base_ref
  5.8 129.9 %shard_map.222 = (bf16[768,2304]{1,0:T(8,128)(2,1)}, bf16[768,768]{1,0:T(8,128)(2,1)}, bf16[1024,2304]{1,0:T(8,128)(2,1)}, bf16[1024,768]{1,0:T(8,128)(2,1)}, f3...) custom-call(f32[1024,768]{1,0:T(8,128)} %residual_ref.3, ...), custom_call_target="tpu_custom_call" | custom-call | flops 12884901888 | bytes 15728640 | tf_op jit(solution)/shard_map/pallas_call | solution.py:1138
  135.7 152.4 %shard_map.223 = (bf16[8,320,768]{2,1,0:T(8,128)(2,1)}, bf16[8,320,768]{2,1,0:T(8,128)(2,1)}, f32[8,8,384]{2,1,0:T(8,128)}, bf16[4,2560,768]{2,1,0:T(8,128)(2,1)...) custom-call(bf16[8,320,768]{2,1,0:T(8,128)(2,1)} %get-tuple-element., ...), custom_call_target="tpu_custom_call" | custom-call | flops 72477573120 | bytes 86507520 | tf_op jit(solution)/shard_map/pallas_call | solution.py:657
  288.0 0.2 convolution_bitcast_fusion
  288.2 0.6 reshape.30.base_ref
  288.9 151.8 %shard_map.224 = (f32[1024,768]{1,0:T(8,128)}, f32[1024,768]{1,0:T(8,128)}, f32[192,2304]{1,0:T(8,128)}, f32[192,768]{1,0:T(8,128)}, f32[24,768]{1,0:T(8,128)}, ...) custom-call(bf16[1024,2304]{1,0:T(8,128)(2,1)} %get-tuple-element.39, ...), custom_call_target="tpu_custom_call" | custom-call | flops 12884901888 | bytes 31457280 | tf_op jit(solution)/shard_map/pallas_call | solution.py:1928
  440.7 1.4 slice_bitcast_fusion
  442.1 1.4 slice_reduce_fusion
  443.5 1.7 fusion
  445.3 3.9 copy.31
  449.2 1.7 copy.32
  450.8 0.9 copy-done.4
  451.8 1.2 copy.33
  453.0 0.2 copy-done.5
  453.2 0.8 copy.34
  454.0 0.4 copy-done.3
  454.5 1.4 copy.35
  455.9 1.4 copy.36
  (12 shorter events, 0.0 us)
Async XLA Ops:
  0.6 3.4 copy-start
  135.7 152.4 %copy-start.7 = (f32[32,768]{1,0:T(8,128)S(1)}, f32[32,768]{1,0:T(8,128)}, u32[]{:S(2)}) copy-start(f32[32,768]{1,0:T(8,128)} %constant.10.clone) | copy-start | bytes 294916
  288.9 154.7 %copy-start.6 = (f32[768,32]{1,0:T(8,128)S(1)}, f32[768,32]{1,0:T(8,128)}, u32[]{:S(2)}) copy-start(f32[768,32]{1,0:T(8,128)} %constant.11.clone) | copy-start | bytes 294916
  445.3 3.9 copy-start.1
  449.2 2.6 copy-start.4
  451.8 1.4 copy-start.5
  451.8 2.7 copy-start.3
  453.2 2.6 copy-start.2

commit v2 on v1

--- a/solution.py
+++ b/solution.py
@@ -399,15 +399,20 @@
 
     pl.semaphore_wait(barrier, members + 1)
 
-    @pl.loop(1, members)
-    def _(step):
+    neighbours = [step for step in range(1, members) if step & (step - 1) == 0]
+    for step in neighbours:
         sending_gates(step).start()
         sending(step).start()
-
     for copy in weight_loads:
         copy.wait()
     own_rows.wait()
     own_gates.wait()
+    sending_gates(1).wait_recv()
+    sending(1).wait_recv()
+    for step in range(1, members):
+        if step not in neighbours:
+            sending_gates(step).start()
+            sending(step).start()
 
     @pl.loop(0, blocks)
     def _(index):
@@ -417,7 +422,7 @@
         def _(place):
             step = index * block_steps + place
 
-            @pl.when(step > 0)
+            @pl.when(step > 1)
             def _():
                 sending_gates(step).wait_recv()
                 sending(step).wait_recv()
@@ -1045,7 +1050,7 @@
 
     keep(7).start()
 
-    logits = dot_nt(router_ref[...], normed2[...])[:members, :]
+    logits = dot_nt(router_ref[...], normed2[...])
     first, second = route_rows[:1, :] == names, route_rows[1:, :] == names
     lean = jnp.sum(jnp.where(first, logits, 0.0), axis=0, keepdims=True)
     lean = lean - jnp.sum(jnp.where(second, logits, 0.0), axis=0, keepdims=True)
@@ -1207,20 +1212,20 @@
     head_dim,
     capacity,
     reduce_here,
-    projected,
     logs,
     row_ref,
     route_rows,
     base_ref,
-    normed,
     normed2,
     merged,
-    projection_full,
     attended_full,
     router_ref,
     gains_ref,
     counts_ref,
     gates_back,
+    projected_ref,
+    normed_ref,
+    projection_ref,
     back_ref,
     out_grad_ref,
     gated_ref,
@@ -1241,6 +1246,9 @@
     distant_in,
     outer_crossed,
     hidden_grad_ref,
+    projected,
+    normed,
+    projection_full,
     mask_ref,
     log_turned,
     dk_total,
@@ -1274,6 +1282,7 @@
     stream_sems,
     distant_sems,
     across_sems,
+    outer_sems,
     near_sems,
     far_sems,
     half_sems,
@@ -1287,8 +1296,9 @@
     result_arrive,
     back_load_sems,
     final_sems,
+    held_sems,
 ):
-    tokens, width = normed.shape
+    tokens, width = normed2.shape
     pairs = width // lanes
     group = width // shards
     expert, shard = lax.axis_index("expert"), lax.axis_index("shard")
@@ -1306,20 +1316,49 @@
     own_columns = pl.ds(pl.multiple_of(top_level * wide, lanes), wide)
     other_columns = pl.ds(pl.multiple_of((1 - top_level) * wide, lanes), wide)
 
-    def distant_copy(matrix, source):
-        top = width // 2 if matrix == 0 else 0
-        return add_remote(
-            source.at[top:, :],
-            distant_in.at[matrix, top:, :],
-            distant_sems.at[0, matrix],
-            distant_sems.at[1, matrix],
+    def inner_remote(source):
+        middle = width // 2
+        return add_remote(
+            source.at[middle:, :],
+            distant_in.at[0, middle:, :],
+            distant_sems.at[0],
+            distant_sems.at[1],
             distant,
         )
 
-    across_copy = add_remote(
-        outer_given, outer_crossed, across_sems.at[0], across_sems.at[1], across
-    )
+    lines_each = width // 4
+
+    def lines_of(index):
+        return slice(index * lines_each, (index + 1) * lines_each)
+
+    def across_copy(index):
+        return add_remote(
+            outer_given.at[lines_of(index), :],
+            outer_crossed.at[lines_of(index), :],
+            across_sems.at[0, index],
+            across_sems.at[1, index],
+            across,
+        )
+
+    def outer_distant(index, source):
+        return add_remote(
+            source.at[lines_of(index), :],
+            distant_in.at[1, lines_of(index), :],
+            outer_sems.at[0, index],
+            outer_sems.at[1, index],
+            distant,
+        )
+
+    def pass_outer(indices):
+        @pl.when(native_here)
+        def _():
+            for index in indices:
+                across_copy(index).wait_recv()
+                outer_distant(index, outer_crossed).start()
+
     part_refs = [attended_part] + [parts.at[index] for index in range(3)]
+    half_width = width // 2
+    part_halves = [((0, 0), (1, 0)), ((2, 0), (0, 1)), ((1, 1), (2, 1))]
     me, device_of = group_place(members, shards)
 
     def result_rows():
@@ -1494,7 +1533,11 @@
                 if index == 0:
                     attended_out[rows, :] = values
                 else:
-                    projection_out[rows, (index - 1) * width : index * width] = values
+                    for place, (kind, side_of) in enumerate(part_halves[index - 1]):
+                        left = kind * width + side_of * half_width
+                        projection_out[rows, left : left + half_width] = values[
+                            :, place * half_width : (place + 1) * half_width
+                        ]
 
     def small_step(stage):
         if reduce_here:
@@ -1504,6 +1547,12 @@
             if stage < 4:
                 small_copy(stage + 1).start()
 
+    held_loads = [
+        pltpu.make_async_copy(source, target, held_sems.at[index])
+        for index, (source, target) in enumerate(
+            [(projected_ref, projected), (normed_ref, normed), (projection_ref, projection_full)]
+        )
+    ]
     barrier = pltpu.get_barrier_semaphore()
     partners = [across, distant]
     if reduce_here:
@@ -1519,16 +1568,18 @@
     own_result.start()
     pl.semaphore_wait(barrier, len(partners) + members - 1)
 
-    across_copy.start()
+    for index in range(4):
+        across_copy(index).start()
 
     @pl.when(native_here)
     def _():
-        distant_copy(0, inner_crossed).start()
+        inner_remote(inner_crossed).start()
 
     @pl.when(jnp.logical_not(native_here))
     def _():
-        distant_copy(0, inner_mine).start()
-        distant_copy(1, outer_mine).start()
+        inner_remote(inner_mine).start()
+        for index in range(4):
+            outer_distant(index, outer_mine).start()
 
     def load_rows(source, target, part, kind):
         return pltpu.make_async_copy(
@@ -1554,7 +1605,7 @@
         )
         for top in range(0, back_count, tokens)
     ]
-    for copy in back_loads:
+    for copy in back_loads + held_loads:
         copy.start()
     for part in range(2):
         load_rows(hidden_ref, first_in, part, 0).start()
@@ -1574,7 +1625,7 @@
         )
     small_own[...] = jnp.zeros_like(small_own)
     bias_top = small_own.shape[0] - pairs * bias_rows.shape[1]
-    lane = lax.broadcasted_iota(jnp.int32, (tile, lanes), 1).astype(f32)
+    lane = lax.broadcasted_iota(jnp.int32, (tile, members), 1).astype(f32)
     for copy in back_loads:
         copy.wait()
 
@@ -1609,7 +1660,7 @@
         above = logit_grad.astype(bf16)
         below = (logit_grad - above.astype(f32)).astype(bf16)
         router_grad = dot_tn(above, values) + dot_tn(below, values)
-        small_own[2:bias_top, :] += router_grad[: bias_top - 2, :]
+        small_own[2 : 2 + members, :] += router_grad
         gradient = dot_nn(above, router_ref[...]) + dot_nn(below, router_ref[...]) + combined
         load_rows(hidden_ref, first_in, part, 0).wait()
         load_rows(out_grad_ref, second_in, part, 1).wait()
@@ -1675,23 +1726,27 @@
     def _(step):
         result_copy(step).start()
 
-    attend(0, pairs // 2)
+    def make_part(index):
+        for place, (kind, side_of) in enumerate(part_halves[index]):
+            left = side_of * half_width
+            sums = dot_tn(normed[...], grads[kind, :, left : left + half_width])
+            parts[index, :, place * half_width : (place + 1) * half_width] = sums.astype(bf16)
+        start_near(index + 1)
+
+    for copy in held_loads:
+        copy.wait()
+    pass_outer(range(2))
+    attend(0, 1)
+    pass_outer(range(2, 4))
+    attend(1, pairs // 2)
+    make_part(0)
     near_to_far(0)
-
-    @pl.when(native_here)
-    def _():
-        across_copy.wait_recv()
-        distant_copy(1, outer_crossed).start()
 
     attend(pairs // 2, pairs)
     far_to_half(0)
-    for index in range(3):
-        @pl.loop(0, width // tile)
-        def _(part):
-            columns = pl.ds(pl.multiple_of(part * tile, tile), tile)
-            parts[index, :, columns] = dot_tn(normed[...], grads[index, :, columns]).astype(bf16)
-
-        start_near(index + 1)
+    near_to_far(1)
+    for index in range(1, 3):
+        make_part(index)
     per_pair = bias_rows.shape[1]
     for pair in range(pairs):
         top = bias_top + pair * per_pair
@@ -1752,10 +1807,15 @@
         @pl.when(jnp.logical_not(native_here))
         def _():
             if matrix == 1:
-                across_copy.wait_recv()
+                for index in range(4):
+                    across_copy(index).wait_recv()
             final_load(matrix, crossed, 0).start()
 
-        distant_copy(matrix, inner_mine).wait_recv()
+        if matrix == 0:
+            inner_remote(inner_mine).wait_recv()
+        else:
+            for index in range(4):
+                outer_distant(index, outer_mine).wait_recv()
         for copy in distant_loads(matrix):
             copy.start()
 
@@ -1797,25 +1857,33 @@
         for copy in final_stores[2:] if matrix == 1 else final_stores[:2]:
             copy.start()
 
-    chunks = range(1, count)
     for part in range(2):
         load_rows(residual_ref, first_in, part, 0).start()
         load_rows(hidden_grad_ref, second_in, part, 1).start()
     half_to_quad(0)
-    for index in chunks:
+    for index in range(2, count):
         near_to_far(index)
-    for part in range(row_parts // 2):
-        norm_rows(part)
+    far_to_half(1)
+    norm_rows(0)
     quad_to_piece(0)
-    for index in chunks:
+    half_to_quad(1)
+    norm_rows(1)
+    for index in range(2, count):
         far_to_half(index)
-    for part in range(row_parts // 2, row_parts):
+    piece_to_finished(0)
+    quad_to_piece(1)
+    norm_rows(2)
+    for index in range(2, count):
+        half_to_quad(index)
+    finished_to_quad(0)
+    piece_to_finished(1)
+    for part in range(3, row_parts):
         norm_rows(part)
     if reduce_here:
         small_copy(0).start()
-    piece_to_finished(0)
-    for index in chunks:
-        half_to_quad(index)
+    for index in range(2, count):
+        quad_to_piece(index)
+    finished_to_quad(1)
     own_result.wait()
 
     @pl.loop(1, members)
@@ -1824,25 +1892,23 @@
 
     block_rows(0)
     small_step(0)
-    for index in chunks:
-        quad_to_piece(index)
-    finished_to_quad(0)
+    for index in range(2, count):
+        piece_to_finished(index)
+    for index in range(2):
+        quad_to_back(index)
     block_rows(1)
     small_step(1)
-    for index in chunks:
-        piece_to_finished(index)
+    for index in range(2, count):
+        finished_to_quad(index)
     start_final(0)
     block_rows(2)
     small_step(2)
-    quad_to_back(0)
-    for index in chunks:
-        finished_to_quad(index)
+    for index in range(2, count):
+        quad_to_back(index)
     for part in range(3, row_parts):
         block_rows(part)
     small_step(3)
     finish_final(0)
-    for index in chunks:
-        quad_to_back(index)
     small_step(4)
     start_final(1)
     finish_final(1)
@@ -1853,14 +1919,19 @@
     else:
         small_out[...] = small_own[...]
         for index in range(3):
-            projection_out[:, index * width : (index + 1) * width] = parts[index]
+            for place, (kind, side_of) in enumerate(part_halves[index]):
+                left = kind * width + side_of * half_width
+                projection_out[:, left : left + half_width] = parts[
+                    index, :, place * half_width : (place + 1) * half_width
+                ]
         attended_out[...] = attended_part[...]
 
     for part in range(row_parts - 2, row_parts):
         store_rows(block_out, part).wait()
-    across_copy.wait_send()
-    for matrix in range(2):
-        distant_copy(matrix, inner_mine).wait_send()
+    inner_remote(inner_mine).wait_send()
+    for index in range(4):
+        across_copy(index).wait_send()
+        outer_distant(index, outer_mine).wait_send()
     for copy in final_stores:
         copy.wait()
     if reduce_here:
@@ -1929,7 +2000,7 @@
         functools.partial(
             back_kernel, shards, members, width // heads, capacity, reduce_here
         ),
-        in_specs=[whole] * 14 + [anywhere] * 10,
+        in_specs=[whole] * 11 + [anywhere] * 13,
         out_specs=[anywhere] * 2 + [whole] * 3 + [anywhere] * 5,
         out_shape=[shape((tokens, width), f32)] * 2
         + sums
@@ -1942,6 +2013,9 @@
             shape((tokens, width), f32),
         ],
         scratch_shapes=[
+            vmem(projected.shape, bf16),
+            vmem(normed.shape, bf16),
+            vmem(projection_full.shape, bf16),
             vmem((span, tokens), f32),
             vmem((lanes, tokens), f32),
             vmem((tokens, lanes), f32),
@@ -1973,8 +2047,9 @@
             vmem((5,) + small_shape, f32),
             vmem((5,) + small_shape, f32),
             dma((3, 2)),
-            dma((2, 2)),
             dma((2,)),
+            dma((2, 4)),
+            dma((2, 4)),
             dma((2, count, 2)),
             dma((2, count)),
             dma((2, count)),
@@ -1988,6 +2063,7 @@
             dma((members,)),
             dma((4,)),
             dma((2, 4)),
+            dma((3,)),
         ],
         compiler_params=pltpu.CompilerParams(
             collective_id=4, has_side_effects=True, vmem_limit_bytes=62 * 2**20
@@ -1998,20 +2074,20 @@
             transcendentals=heads * tokens * tokens // 2,
         ),
     )(
-        projected,
         logs,
         marks[None, :],
         route_rows,
         base_turned.reshape(pairs, per_pair, span),
-        normed,
         normed2,
         merged,
-        projection_full,
         attended_full,
         router,
         gains,
         counts,
         gates_back,
+        projected,
+        normed,
+        projection_full,
         back,
         out_grad,
         gated,
@@ -2055,7 +2131,7 @@
     table_rows, table_turned = bias_tables(buckets)
 
     gains = jnp.stack([norm1_gain, norm2_gain])
-    router = jnp.pad(w_router.T, ((0, -experts_all % lanes), (0, 0)))
+    router = w_router.T
     route_rows = routes.T
     base_rows = jnp.dot(rel_bias, table_rows.T, precision=highest)
     base_turned = jnp.dot(rel_bias, table_turned.T, precision=highest)

time: 466 us -> 453 us (0.972)
  Pallas kernels: 434 us -> 423 us
    pallas_call x1, Pallas kernels: 152 us -> 139 us  [run_experts(): pl.pallas_call(functools.partial(expert_kernel, shards), in_specs=[anywhe...]
where the time goes in v2:
time: 453 us; the launch traced here: 445 us
  Pallas kernels  423 us (93%)
  local copies, waits for them, and re-layouts  17.5 us (4%)
    pallas_call x1, Pallas kernels, run_back(): pl.pallas_call(functools.partial(back_kernel, shards, members, width // h...  154 us
    pallas_call x1, Pallas kernels, run_experts(): pl.pallas_call(functools.partial(expert_kernel, shards), in_specs=[anywhe...  139 us
    pallas_call x1, Pallas kernels, run_front(): pl.pallas_call(functools.partial(front_kernel, shards, width // heads), i...  130 us
    unnamed x22, local copies, waits for them, and re-layouts  12 us

profile of v2, /device:TPU:0, one launch (start us, length us, event | category | flops | bytes accessed | tf_op | source)
XLA Modules:
  0.0 444.9 jit_solution(5399186588712724937)
XLA Ops:
  0.6 0.0 copy-start
  0.7 0.7 stack.10
  1.4 0.7 stack.9
  2.0 0.6 pad_maximum_fusion.gains_ref
  2.6 1.1 convolution_bitcast_fusion.1
  3.7 0.6 reshape.29.base_ref
  4.4 129.8 %shard_map.222 = (bf16[768,2304]{1,0:T(8,128)(2,1)}, bf16[768,768]{1,0:T(8,128)(2,1)}, bf16[1024,2304]{1,0:T(8,128)(2,1)}, bf16[1024,768]{1,0:T(8,128)(2,1)}, f3...) custom-call(f32[1024,768]{1,0:T(8,128)} %residual_ref.3, ...), custom_call_target="tpu_custom_call" | custom-call | flops 12884901888 | bytes 15728640 | tf_op jit(solution)/shard_map/pallas_call | solution.py:1143
  134.2 0.0 copy-start.7
  134.2 139.1 %shard_map.223 = (bf16[8,320,768]{2,1,0:T(8,128)(2,1)}, bf16[8,320,768]{2,1,0:T(8,128)(2,1)}, f32[8,8,384]{2,1,0:T(8,128)}, bf16[4,2560,768]{2,1,0:T(8,128)(2,1)...) custom-call(bf16[8,320,768]{2,1,0:T(8,128)(2,1)} %get-tuple-element., ...), custom_call_target="tpu_custom_call" | custom-call | flops 72477573120 | bytes 86507520 | tf_op jit(solution)/shard_map/pallas_call | solution.py:662
  273.4 0.2 convolution_bitcast_fusion
  273.5 0.6 reshape.30.base_ref
  274.2 153.6 %shard_map.224 = (f32[1024,768]{1,0:T(8,128)}, f32[1024,768]{1,0:T(8,128)}, f32[192,2304]{1,0:T(8,128)}, f32[192,768]{1,0:T(8,128)}, f32[24,768]{1,0:T(8,128)}, ...) custom-call(f32[1024,128]{1,0:T(8,128)} %get-tuple-element.39.logs, ...), custom_call_target="tpu_custom_call" | custom-call | flops 12884901888 | bytes 31457280 | tf_op jit(solution)/shard_map/pallas_call | solution.py:1999
  427.8 1.4 slice_bitcast_fusion
  429.2 1.4 slice_reduce_fusion
  430.6 1.7 fusion
  432.4 3.9 copy.31
  436.3 1.7 copy.32
  437.9 0.9 copy-done.4
  438.9 1.2 copy.33
  440.1 0.2 copy-done.5
  440.3 0.8 copy.34
  441.1 0.4 copy-done.3
  441.6 1.4 copy.35
  443.0 1.4 copy.36
  (11 shorter events, 0.0 us)
Async XLA Ops:
  0.6 2.0 copy-start
  134.2 139.1 %copy-start.7 = (f32[32,768]{1,0:T(8,128)S(1)}, f32[32,768]{1,0:T(8,128)}, u32[]{:S(2)}) copy-start(f32[32,768]{1,0:T(8,128)} %constant.7.clone) | copy-start | bytes 294916
  274.2 156.5 %copy-start.6 = (f32[768,32]{1,0:T(8,128)S(1)}, f32[768,32]{1,0:T(8,128)}, u32[]{:S(2)}) copy-start(f32[768,32]{1,0:T(8,128)} %constant.8.clone) | copy-start | bytes 294916
  432.4 3.9 copy-start.1
  436.3 2.6 copy-start.4
  438.9 1.4 copy-start.5
  438.9 2.7 copy-start.3
  440.3 2.6 copy-start.2
